TPU v7x, 128 devices: a whole 4x4x4 slice. The times are simulated.
128 devices in a mesh: dp: 32 (over y, z, core), tensor: 4 (over x).
Axes of the slice: x: 4, y: 4, z: 4, core: 2. Of those that a mesh axis runs over, the one named last changes fastest.
Arguments:
- gradient: bfloat16 [4, 1, 512, 16384], P('tensor', None, 'dp'), may hold values from -6 to 6
- slot_block: int32 [4, 64], P('tensor'), may hold values from -1 to 31, as said below
- refresh_target: int32 [256], replicated, may hold values from -1 to 127, as said below
- first_moment: float32 [4, 64, 512, 512], P('tensor', 'dp'), may hold values from -6 to 6
- second_moment: float32 [4, 64, 512, 512], P('tensor', 'dp'), may hold values from 0.1 to 2
- left_gram: float32 [4, 64, 512, 512], P('tensor', 'dp'), as said below
- right_gram: float32 [4, 64, 512, 512], P('tensor', 'dp'), as said below
- left_basis: float32 [4, 64, 512, 512], P('tensor', 'dp'), as said below
- right_basis: float32 [4, 64, 512, 512], P('tensor', 'dp'), as said below
Outputs:
- update: float32 [4, 64, 512, 512], P('tensor', 'dp')
- new_left_basis: float32 [4, 64, 512, 512], P('tensor', 'dp')
- new_right_basis: float32 [4, 64, 512, 512], P('tensor', 'dp')
Inputs may be any that keep to these rules, and one draw needn't show every extreme that they name: `slot_block`: blocks of a tensor index are numbered r * 32 + c; each of the 32 blocks is held by exactly one slot of that tensor index, -1 marks an empty slot. An owner's blocks fill its first slots; 16 owners of each tensor index hold blocks, all of them but at most one in all 2 slots, the other owners none. `refresh_target`: entry (g * 4 + t) * 2 + s belongs to slot s of the device at dp index g and tensor index t. It is -1, or h * 4 + u for the device at dp index h and tensor index u that refreshes that slot. Exactly 32 entries are not -1; they lie in slots that hold a block and name distinct devices that hold no block. The last device holds no block and is always named. `left_gram`: each matrix is symmetric positive definite. `right_gram`: each matrix is symmetric positive definite. `left_basis`: each matrix is invertible. `right_basis`: each matrix is invertible.
All inputs are finite; a program needn't handle non-finite values.
Results may differ from a plain program's by a relative error of at most 0.0003.
Values may be sent and summed in bfloat16 or wider, within the bound.
No kernel may reach another device: no remote copies, remote signals or barrier semaphores. Data moves between devices by JAX's collectives and lax.ppermute only.
A program may use at most 128 MiB of HBM per device.

v0:
```python
import jax
import jax.numpy as jnp
from jax import lax
from jax.sharding import PartitionSpec as P

SWEEPS = 2


highest = lax.Precision.HIGHEST


def orthonormal(gram_stack, basis_stack):
    basis = basis_stack
    for sweep_index in range(SWEEPS):
        image = jnp.einsum("bik,bkj->bij", gram_stack, basis, precision=highest)
        inner = jnp.einsum("bki,bkj->bij", image, image, precision=highest)
        factor = jnp.linalg.cholesky(inner)
        basis = lax.linalg.triangular_solve(
            factor, image, left_side=False, lower=True, transpose_a=True
        )
    return basis


def local(
    gradient,
    slot_block,
    refresh_target,
    first_moment,
    second_moment,
    left_gram,
    right_gram,
    left_basis,
    right_basis,
):
    dp_size = lax.axis_size("dp")
    tensor_size = lax.axis_size("tensor")
    devices = dp_size * tensor_size
    dp_index = lax.axis_index("dp")
    self_index = dp_index * tensor_size + lax.axis_index("tensor")
    slots = first_moment.shape[1]
    block = first_moment.shape[2]
    row_blocks = gradient.shape[1]
    slab_rows = gradient.shape[2]
    columns = gradient.shape[3] // block
    blocks_view = gradient[0].reshape(row_blocks, slab_rows, columns, block).transpose(0, 2, 1, 3)
    blocks_view = blocks_view.reshape(row_blocks * columns, slab_rows, block)
    slot_table = slot_block[0]
    picked = jnp.take(blocks_view, jnp.maximum(slot_table, 0), axis=0)
    picked = jnp.where((slot_table >= 0)[:, None, None], picked, jnp.zeros_like(picked))
    outbox = picked.reshape(dp_size, slots, slab_rows, block)
    grads = lax.all_to_all(outbox, "dp", split_axis=0, concat_axis=2, tiled=True)[0]
    occupied = lax.dynamic_slice_in_dim(slot_table, dp_index * slots, slots) >= 0
    wanted = lax.dynamic_slice_in_dim(refresh_target, self_index * slots, slots) >= 0
    left_old = left_basis[0]
    right_old = right_basis[0]
    left_new = 0.95 * left_gram[0] + 0.05 * jnp.einsum(
        "sik,sjk->sij", grads, grads, preferred_element_type=jnp.float32
    )
    right_new = 0.95 * right_gram[0] + 0.05 * jnp.einsum(
        "ski,skj->sij", grads, grads, preferred_element_type=jnp.float32
    )
    wide = grads.astype(jnp.float32)
    partial_rot = jnp.einsum("ski,skj->sij", left_old, wide, precision=highest)
    rotated = jnp.einsum("sik,skj->sij", partial_rot, right_old, precision=highest)
    moment = 0.9 * first_moment[0] + 0.1 * rotated
    second = 0.95 * second_moment[0] + 0.05 * rotated * rotated
    normed = moment / (jnp.sqrt(second) + 1e-08)
    partial_back = jnp.einsum("sik,skj->sij", left_old, normed, precision=highest)
    update = jnp.einsum("sik,sjk->sij", partial_back, right_old, precision=highest)
    update = jnp.where(occupied[:, None, None], update, jnp.zeros_like(update))
    piece_rows = block // devices
    payload = jnp.stack([left_new, right_new, left_old, right_old], axis=1)
    payload = payload.reshape(slots, 4, devices, piece_rows, block).transpose(2, 0, 1, 3, 4)
    arrived = lax.all_to_all(payload, ("dp", "tensor"), split_axis=0, concat_axis=0, tiled=True)
    arrived = arrived.reshape(devices * slots, 4, piece_rows, block)
    helper_ids = jnp.arange(devices, dtype=jnp.int32)
    slot_ids = jnp.arange(devices * slots, dtype=jnp.int32)
    matches = refresh_target[None, :] == helper_ids[:, None]
    source = jnp.sum(jnp.where(matches, slot_ids[None, :] + 1, 0), axis=1) - 1
    chosen = jnp.take(arrived, jnp.maximum(source, 0), axis=0)
    gathered = lax.all_to_all(chosen, ("dp", "tensor"), split_axis=0, concat_axis=2, tiled=True)[0]
    active = jnp.take(source, self_index) >= 0
    identity = jnp.eye(block, dtype=jnp.float32)
    factors = jnp.where(active, gathered, identity[None])
    both = orthonormal(factors[0:2], factors[2:4])
    result = both.reshape(2, devices, piece_rows, block).transpose(1, 0, 2, 3)
    spread = lax.all_to_all(result, ("dp", "tensor"), split_axis=0, concat_axis=0, tiled=True)
    homes = jnp.take(spread, jnp.maximum(refresh_target, 0), axis=0)
    homes = homes.reshape(devices, slots, 2, piece_rows, block)
    returned = lax.all_to_all(homes, ("dp", "tensor"), split_axis=0, concat_axis=3, tiled=True)[0]
    fresh_left = returned[:, 0]
    fresh_right = returned[:, 1]
    new_left = jnp.where(wanted[:, None, None], fresh_left, left_old)
    new_right = jnp.where(wanted[:, None, None], fresh_right, right_old)
    return (update[None], new_left[None], new_right[None])


def solution(mesh):
    placed = (
        P("tensor", None, "dp", None),
        P("tensor", None),
        P(),
        P("tensor", "dp", None, None),
        P("tensor", "dp", None, None),
        P("tensor", "dp", None, None),
        P("tensor", "dp", None, None),
        P("tensor", "dp", None, None),
        P("tensor", "dp", None, None),
    )
    return jax.shard_map(
        local,
        mesh=mesh,
        in_specs=placed,
        out_specs=(
            P("tensor", "dp", None, None),
            P("tensor", "dp", None, None),
            P("tensor", "dp", None, None),
        ),
        check_vma=False,
    )
```

profile of v0, /device:TPU:3, one launch (start us, length us, event | category | flops | bytes accessed | tf_op | source)
XLA Modules:
  0.0 1007.0 jit_solution(4070646680273387966)
XLA Ops:
  5.5 8.8 all-to-all-start
  18.9 12.3 %all-to-all-done = bf16[32,2,16,512]{3,2,1,0:T(8,128)(2,1)S(1)} async-done(((bf16[32,2,16,512]{3,2,1,0:T(8,128)(2,1)}), bf16[32,2,16,512]{3,2,1,0:T(8,128)(2,1)S(1)}, u32[]{:S(2)}, u32[]{:S(2)}) %all-to-all-start) | async-done | bytes 1048608 | tf_op jit(solution)/shard_map/all_to_all | solution.py:51
  39.0 3.7 bitcast_add_fusion.2
  45.7 7.7 copy_bitcast_fusion
  53.4 6.5 all-to-all-start.1
  60.0 100.3 %all-to-all-done.1 = f32[128,2,4,4,512]{4,3,2,1,0:T(4,128)} async-done(((f32[128,2,4,4,512]{4,3,2,1,0:T(4,128)}), f32[128,2,4,4,512]{4,3,2,1,0:T(4,128)}, u32[]{:S(2)}, u32[]{:S(2)}) %all-to-all-start.1) | async-done | bytes 8388640 | tf_op jit(solution)/shard_map/all_to_all | solution.py:74
  160.4 8.1 gather_fusion.1
  168.5 5.1 broadcast_select_fusion.2
  173.7 9.9 all-to-all-start.2
  187.1 48.4 %all-to-all-done.2 = f32[128,4,4,512]{3,2,1,0:T(4,128)} async-done(((f32[128,4,4,512]{3,2,1,0:T(4,128)}), f32[128,4,4,512]{3,2,1,0:T(4,128)}, u32[]{:S(2)}, u32[]{:S(2)}) %all-to-all-start.2) | async-done | bytes 4194336 | tf_op jit(solution)/shard_map/all_to_all | solution.py:81
  235.5 5.0 copy.186
  240.4 5.3 squeeze.29
  247.6 3.8 fusion.8
  252.7 5.0 fusion.113
  265.3 24.7 %custom-call.35 = f32[2,128,128]{2,1,0:T(8,128)S(1)} custom-call(f32[2,128,128]{2,1,0:T(8,128)} %cholesky.430), custom_call_target="Cholesky" | custom-call | tf_op jit(solution)/shard_map/jit(cholesky)/cholesky | solution.py:17
  290.7 21.1 %custom-call.36 = f32[2,1,128,128]{2,3,1,0:T(8,128)} custom-call(f32[2,1,128,128]{3,2,1,0:T(8,128)} %select_bitcast_fusion.6), custom_call_target="InvertDiagBlocksLowerTriangular" | custom-call | tf_op jit(solution)/shard_map/jit(cholesky)/cholesky | solution.py:17
  318.5 24.9 %custom-call.37 = f32[2,128,128]{2,1,0:T(8,128)} custom-call(f32[2,128,128]{2,1,0:T(8,128)} %cholesky.434), custom_call_target="Cholesky" | custom-call | tf_op jit(solution)/shard_map/jit(cholesky)/cholesky | solution.py:17
  345.1 21.3 %custom-call.38 = f32[2,1,128,128]{2,3,1,0:T(8,128)} custom-call(f32[2,1,128,128]{3,2,1,0:T(8,128)} %get-tuple-element.72), custom_call_target="InvertDiagBlocksLowerTriangular" | custom-call | tf_op jit(solution)/shard_map/jit(cholesky)/cholesky | solution.py:17
  371.5 24.9 %custom-call.39 = f32[2,128,128]{2,1,0:T(8,128)} custom-call(f32[2,128,128]{2,1,0:T(8,128)} %cholesky.439), custom_call_target="Cholesky" | custom-call | tf_op jit(solution)/shard_map/jit(cholesky)/cholesky | solution.py:17
  398.0 21.1 %custom-call.40 = f32[2,1,128,128]{2,3,1,0:T(8,128)} custom-call(f32[2,1,128,128]{3,2,1,0:T(8,128)} %get-tuple-element.70), custom_call_target="InvertDiagBlocksLowerTriangular" | custom-call | tf_op jit(solution)/shard_map/jit(cholesky)/cholesky | solution.py:17
  423.4 24.9 %custom-call.41 = f32[2,128,128]{2,1,0:T(8,128)} custom-call(f32[2,128,128]{2,1,0:T(8,128)} %convolution_subtract_fusion.9), custom_call_target="Cholesky" | custom-call | tf_op jit(solution)/shard_map/jit(cholesky)/cholesky | solution.py:17
  454.6 14.2 %while.5 = (s32[]{:T(128)}, f32[2,512,512]{2,1,0:T(8,128)}, s32[4,2]{0,1:T(2,128)S(1)}, f32[4,2,128,128]{3,2,0,1:T(8,128)}, s32[]{:T(128)}) while((s32[]{:T(128)}, f32[2,512,512]{2,1,0:T(8,128)}, s32[4,2]{0,1:T(2,128)S(1)}, f32[4,2,128,128]{3,2,0,1:T(8,128)}, s32[]{:T(128)}) %tuple.64), condition=%wide.while_cond, body=%wide.while_body.sunk | while | flops 2 | bytes 263777 | solution.py:18
  468.8 80.4 %custom-call.42 = f32[2,4,128,128]{2,3,1,0:T(8,128)} custom-call(f32[2,4,128,128]{3,2,1,0:T(8,128)} %bitcast.223), custom_call_target="InvertDiagBlocksLowerTriangular" | custom-call | tf_op jit(solution)/shard_map/triangular_solve/custom-call.3 | solution.py:18
  557.5 4.1 fusion.48
  562.2 3.8 fusion.10
  567.4 5.2 fusion.114
  580.2 24.3 %custom-call.43 = f32[2,128,128]{2,1,0:T(8,128)S(1)} custom-call(f32[2,128,128]{2,1,0:T(8,128)} %cholesky.443), custom_call_target="Cholesky" | custom-call | tf_op jit(solution)/shard_map/jit(cholesky)/cholesky | solution.py:17
  606.7 21.1 %custom-call.44 = f32[2,1,128,128]{2,3,1,0:T(8,128)} custom-call(f32[2,1,128,128]{3,2,1,0:T(8,128)} %select_bitcast_fusion.3), custom_call_target="InvertDiagBlocksLowerTriangular" | custom-call | tf_op jit(solution)/shard_map/jit(cholesky)/cholesky | solution.py:17
  632.9 25.1 %custom-call.45 = f32[2,128,128]{2,1,0:T(8,128)} custom-call(f32[2,128,128]{2,1,0:T(8,128)} %cholesky.447), custom_call_target="Cholesky" | custom-call | tf_op jit(solution)/shard_map/jit(cholesky)/cholesky | solution.py:17
  659.6 21.1 %custom-call.46 = f32[2,1,128,128]{2,3,1,0:T(8,128)} custom-call(f32[2,1,128,128]{3,2,1,0:T(8,128)} %get-tuple-element.67), custom_call_target="InvertDiagBlocksLowerTriangular" | custom-call | tf_op jit(solution)/shard_map/jit(cholesky)/cholesky | solution.py:17
  685.9 24.9 %custom-call.47 = f32[2,128,128]{2,1,0:T(8,128)} custom-call(f32[2,128,128]{2,1,0:T(8,128)} %cholesky.452), custom_call_target="Cholesky" | custom-call | tf_op jit(solution)/shard_map/jit(cholesky)/cholesky | solution.py:17
  712.5 21.5 %custom-call.48 = f32[2,1,128,128]{2,3,1,0:T(8,128)} custom-call(f32[2,1,128,128]{3,2,1,0:T(8,128)} %get-tuple-element.65), custom_call_target="InvertDiagBlocksLowerTriangular" | custom-call | tf_op jit(solution)/shard_map/jit(cholesky)/cholesky | solution.py:17
  738.2 24.9 %custom-call.49 = f32[2,128,128]{2,1,0:T(8,128)} custom-call(f32[2,128,128]{2,1,0:T(8,128)} %convolution_subtract_fusion.8), custom_call_target="Cholesky" | custom-call | tf_op jit(solution)/shard_map/jit(cholesky)/cholesky | solution.py:17
  769.6 14.6 %while.6 = (s32[]{:T(128)}, f32[2,512,512]{2,1,0:T(8,128)}, s32[4,2]{0,1:T(2,128)S(1)}, f32[4,2,128,128]{3,2,0,1:T(8,128)}, s32[]{:T(128)}) while((s32[]{:T(128)}, f32[2,512,512]{2,1,0:T(8,128)}, s32[4,2]{0,1:T(2,128)S(1)}, f32[4,2,128,128]{3,2,0,1:T(8,128)}, s32[]{:T(128)}) %tuple.70), condition=%wide.while_cond.clone, body=%wide.while_body.clone.sunk | while | flops 2 | bytes 263777 | solution.py:18
  784.1 80.2 %custom-call.50 = f32[2,4,128,128]{2,3,1,0:T(8,128)} custom-call(f32[2,4,128,128]{3,2,1,0:T(8,128)} %bitcast.222), custom_call_target="InvertDiagBlocksLowerTriangular" | custom-call | tf_op jit(solution)/shard_map/triangular_solve/custom-call.3 | solution.py:18
  872.5 3.8 fusion.45
  878.4 4.1 copy.220
  886.0 6.0 all-to-all-start.3
  892.2 29.4 %all-to-all-done.3 = f32[128,2,4,512]{3,2,1,0:T(4,128)} async-done(((f32[128,2,4,512]{3,2,1,0:T(4,128)}), f32[128,2,4,512]{3,2,1,0:T(4,128)}, u32[]{:S(2)}, u32[]{:S(2)}) %all-to-all-start.3) | async-done | bytes 2097184 | tf_op jit(solution)/shard_map/all_to_all | solution.py:87
  921.7 6.3 gather_fusion.2
  928.0 4.1 broadcast_select_fusion
  932.1 6.2 all-to-all-start.4
  945.5 4.9 fusion.4
  950.5 5.1 select_bitcast_fusion
  955.6 34.6 %all-to-all-done.4 = f32[128,2,2,4,512]{4,3,2,1,0:T(4,128)} async-done(((f32[128,2,2,4,512]{4,3,2,1,0:T(4,128)}), f32[128,2,2,4,512]{4,3,2,1,0:T(4,128)}, u32[]{:S(2)}, u32[]{:S(2)}) %all-to-all-start.4) | async-done | bytes 4194336 | tf_op jit(solution)/shard_map/all_to_all | solution.py:90
  990.3 5.0 copy.222
  995.2 5.3 squeeze.30
  1000.5 6.1 fusion.6
  (172 shorter events, 154.3 us)
Async XLA Ops:
  5.5 25.7 %all-to-all-start = ((bf16[32,2,16,512]{3,2,1,0:T(8,128)(2,1)}), bf16[32,2,16,512]{3,2,1,0:T(8,128)(2,1)S(1)}, u32[]{:S(2)}, u32[]{:S(2)}) async-start(bf16[32,2,16,512]{3,2,1,0:T(8,128)(2,1)} %select_select_fusion.2), calls=%async_computation | async-start | bytes 2097152 | tf_op jit(solution)/shard_map/all_to_all | solution.py:51
  14.3 3.0 copy-start.2
  31.2 1.0 copy-start.10
  32.2 1.9 copy-start.11
  53.4 6.5 copy-start.21
  53.4 107.0 %all-to-all-start.1 = ((f32[128,2,4,4,512]{4,3,2,1,0:T(4,128)}), f32[128,2,4,4,512]{4,3,2,1,0:T(4,128)}, u32[]{:S(2)}, u32[]{:S(2)}) async-start(f32[128,2,4,4,512]{4,3,2,1,0:T(4,128)} %copy_bitcast_fusion), calls=%async_computation.1 | async-start | bytes 16777216 | tf_op jit(solution)/shard_map/all_to_all | solution.py:74
  173.7 61.8 %all-to-all-start.2 = ((f32[128,4,4,512]{3,2,1,0:T(4,128)}), f32[128,4,4,512]{3,2,1,0:T(4,128)}, u32[]{:S(2)}, u32[]{:S(2)}) async-start(f32[128,4,4,512]{3,2,1,0:T(4,128)} %broadcast_select_fusion.2), calls=%async_computation.2 | async-start | bytes 8388608 | tf_op jit(solution)/shard_map/all_to_all | solution.py:81
  247.6 3.8 copy-start
  251.4 1.3 copy-start.3
  263.3 1.3 copy-start.9
  311.8 1.6 copy-start.18
  317.1 0.8 copy-start.12
  370.2 0.7 copy-start.15
  450.4 3.3 copy-start.26
  468.8 88.0 %copy-start.19 = (s32[4,2]{0,1:T(2,128)}, s32[4,2]{0,1:T(2,128)S(1)}, u32[]{:S(2)}) copy-start(s32[4,2]{0,1:T(2,128)S(1)} %get-tuple-element.185) | copy-start | bytes 100
  549.3 4.1 copy-start.16
  549.3 4.7 copy-start.4
  556.9 5.4 copy-start.1
  566.1 1.3 copy-start.5
  578.2 1.3 copy-start.8
  631.5 0.7 copy-start.13
  684.6 0.7 copy-start.14
  765.4 4.2 copy-start.20
  864.3 4.1 copy-start.17
  864.3 4.7 copy-start.6
  886.0 6.0 copy-start.22
  886.0 35.7 %all-to-all-start.3 = ((f32[128,2,4,512]{3,2,1,0:T(4,128)}), f32[128,2,4,512]{3,2,1,0:T(4,128)}, u32[]{:S(2)}, u32[]{:S(2)}) async-start(f32[128,2,4,512]{3,2,1,0:T(4,128)} %bitcast.216), calls=%async_computation.3 | async-start | bytes 4194304 | tf_op jit(solution)/shard_map/all_to_all | solution.py:87
  932.1 6.3 copy-start.25
  932.1 58.2 %all-to-all-start.4 = ((f32[128,2,2,4,512]{4,3,2,1,0:T(4,128)}), f32[128,2,2,4,512]{4,3,2,1,0:T(4,128)}, u32[]{:S(2)}, u32[]{:S(2)}) async-start(f32[128,2,2,4,512]{4,3,2,1,0:T(4,128)} %broadcast_select_fusion), calls=%async_computation.4 | async-start | bytes 8388608 | tf_op jit(solution)/shard_map/all_to_all | solution.py:90
  941.9 3.6 copy-start.7
  941.9 3.6 copy-start.23
  941.9 3.6 copy-start.24
where the time goes:
time: 1020 us; the launch traced here: 1010 us
  other arithmetic  542 us (53%)
  waiting for transfers between devices  225 us (22%)
  local copies, waits for them, and re-layouts  110 us (11%)
  matrix products  89.9 us (9%)
  starting transfers between devices  37.4 us (4%)
    another operation x32, other arithmetic, orthonormal(): factor = jnp.linalg.cholesky(inner)  338 us
    another operation x7, other arithmetic, orthonormal(): lax.linalg.triangular_solve(factor, image, left_side=False, lower=True, t...  169 us
    all_to_all x1, waiting for transfers between devices, local(): lax.all_to_all(payload, ('dp', 'tensor'), split_axis=0, concat_axis=0, ti...  100 us
    all_to_all x1, waiting for transfers between devices, local(): lax.all_to_all(chosen, ('dp', 'tensor'), split_axis=0, concat_axis=2, til...  48.4 us
    all_to_all x1, waiting for transfers between devices, local(): lax.all_to_all(homes, ('dp', 'tensor'), split_axis=0, concat_axis=3, tile...  34.6 us
    another operation x28, local copies, waits for them, and re-layouts, orthonormal(): lax.linalg.triangular_solve(factor, image, left_side=False, lower=True, t...  34.6 us
    all_to_all x1, waiting for transfers between devices, local(): lax.all_to_all(result, ('dp', 'tensor'), split_axis=0, concat_axis=0, til...  29.4 us
    another operation x14, matrix products, orthonormal(): lax.linalg.triangular_solve(factor, image, left_side=False, lower=True, t...  25.4 us
  transfers between devices with their start and end apart: 5, of which 5 were waited for; matrix products, arithmetic and copies ran while one was open for 2% of the time, Pallas kernels for 0%

commit v1 on v0

v1 whole, which is shorter than its diff:
```python
import functools

import jax
import jax.numpy as jnp
from jax import lax
from jax.experimental import pallas as pl
from jax.experimental.pallas import tpu as pltpu
from jax.sharding import PartitionSpec as P

BLOCK = 512
PANEL = 128
LEAF = 32
SLOTS = 2
MATS = 2 * SLOTS
CHUNK = 256
WORST = 17.0

f32 = jnp.float32
bf16 = jnp.bfloat16

NN = (((1,), (0,)), ((), ()))
NT = (((1,), (1,)), ((), ()))
TN = (((0,), (0,)), ((), ()))


def split(x):
    high = x.astype(bf16)
    return high, (x - high.astype(f32)).astype(bf16)


def dot(a, b, dims=NN):
    return lax.dot_general(a, b, dims, preferred_element_type=f32)


def dot3(a, b, dims=NN):
    return dot(a[0], b[0], dims) + (dot(a[0], b[1], dims) + dot(a[1], b[0], dims))


def unit_rows(x):
    return x * lax.rsqrt(jnp.sum(x * x, axis=1, keepdims=True))


def leaf(tiles):
    lane = lax.broadcasted_iota(jnp.int32, (8, 128), 1)
    row = lax.broadcasted_iota(jnp.int32, (8, 128), 0)
    within = lane % LEAF
    base = lane - within
    worst = jnp.zeros((1, 128), f32)
    tiles = list(tiles)
    for j in range(LEAF):
        t0, r0 = divmod(j, 8)
        source = base + j
        columns = [None] * t0 + [jnp.take_along_axis(tiles[t], source, axis=1) for t in range(t0, LEAF // 8)]
        inverse = lax.rsqrt(columns[t0][r0 : r0 + 1, :])
        worst = jnp.maximum(worst, jnp.where(inverse < WORST, 0.0, 1.0))
        pivot_row = tiles[t0][r0 : r0 + 1, :] + jnp.where(within[:1] == j, 1.0, 0.0)
        scaled = pivot_row * inverse
        for t in range(t0, LEAF // 8):
            factor = columns[t] * inverse
            if t == t0:
                factor = jnp.where(row > r0, factor, 0.0)
            tiles[t] = tiles[t] - factor * scaled
        own = jnp.where(within[:1] == j, inverse, scaled)
        tiles[t0] = jnp.where(row == r0, own, tiles[t0])
    for t in range(LEAF // 8):
        tiles[t] = jnp.where(within <= row + 8 * t, tiles[t], 0.0)
    return tiles, worst


def factor_panels(work, worst_ref):
    lane = lax.broadcasted_iota(jnp.int32, (LEAF, PANEL), 1)
    row = lax.broadcasted_iota(jnp.int32, (LEAF, PANEL), 0)
    for b in range(PANEL // LEAF):
        top = b * LEAF
        rows = slice(top, top + LEAF)
        packed = jnp.concatenate([work[m, rows, rows] for m in range(MATS)], axis=1)
        tiles, worst = leaf([packed[8 * t : 8 * t + 8] for t in range(LEAF // 8)])
        worst_ref[...] = jnp.maximum(worst_ref[...], worst)
        packed = jnp.concatenate(tiles, axis=0)
        below = PANEL - top - LEAF
        for m in range(MATS):
            inverse = split(packed[:, m * LEAF : (m + 1) * LEAF])
            band = jnp.where(lane - top == row, 1.0, jnp.where((lane >= top) & (lane < top + LEAF), 0.0, work[m, rows, :]))
            band = dot3(inverse, split(band))
            if below:
                under = slice(top + LEAF, PANEL)
                old = work[m, under, :]
                factor = dot3(split(old[:, rows]), inverse, NT)
                wide_lane = lax.broadcasted_iota(jnp.int32, (below, PANEL), 1)
                kept = jnp.where((wide_lane >= top) & (wide_lane < top + LEAF), 0.0, old)
                work[m, under, :] = kept - dot3(split(factor), split(band))
            work[m, rows, :] = band
    full_lane = lax.broadcasted_iota(jnp.int32, (PANEL, PANEL), 1)
    full_row = lax.broadcasted_iota(jnp.int32, (PANEL, PANEL), 0)
    for m in range(MATS):
        work[m] = jnp.where(full_lane <= full_row, work[m], 0.0)


def orthonormal_rows(z, work, worst_ref):
    for p in range(BLOCK // PANEL):
        rows = pl.ds(p * PANEL, PANEL)

        @pl.loop(0, MATS)
        def _(m):
            part = split(z[m, rows, :])
            work[m] = dot3(part, part, NT)

        factor_panels(work, worst_ref)

        @pl.loop(0, MATS)
        def _(m):
            fresh = dot3(split(work[m]), split(z[m, rows, :]))
            z[m, rows, :] = fresh
            if p + 1 < BLOCK // PANEL:
                rest = pl.ds((p + 1) * PANEL, BLOCK - (p + 1) * PANEL)
                fresh = split(fresh)
                old = z[m, rest, :]
                along = dot3(split(old), fresh, NT)
                z[m, rest, :] = old - dot3(split(along), fresh)


def step_kernel(
    held, wanted, grads, first, second, left_gram, right_gram, left, right,
    update, new_left, new_right, z, a_high, a_low, work, worst_ref, temp,
):
    @pl.loop(0, SLOTS)
    def _(s):
        new_left[s] = left[s]
        new_right[s] = right[s]

        @pl.when(held[s] == 0)
        def _():
            update[s] = jnp.zeros((BLOCK, BLOCK), f32)

        @pl.when(held[s] != 0)
        def _():
            g = grads[:, s].reshape(BLOCK, BLOCK)
            r = split(right[s])
            turned = split(left[s].T)
            temp[...] = dot(turned[0], g) + dot(turned[1], g)
            for c in range(0, BLOCK, CHUNK):
                rows = pl.ds(c, CHUNK)
                rotated = dot3(split(temp[rows, :]), r)
                moment = 0.9 * first[s, rows, :] + 0.1 * rotated
                spread = 0.95 * second[s, rows, :] + 0.05 * rotated * rotated
                temp[rows, :] = moment / (jnp.sqrt(spread) + 1e-08)
            normed = split(temp[...])
            for c in range(0, BLOCK, CHUNK):
                rows = pl.ds(c, CHUNK)
                back = dot3(split(left[s, rows, :]), normed)
                update[s, rows, :] = dot3(split(back), r, NT)

    @pl.when((wanted[0] + wanted[1]) != 0)
    def _():
        @pl.loop(0, SLOTS)
        def _(s):
            g = grads[:, s].reshape(BLOCK, BLOCK)
            gt = g.T
            for side, gram in enumerate((left_gram, right_gram)):
                m = SLOTS * s + side
                for c in range(0, BLOCK, CHUNK):
                    rows = pl.ds(c, CHUNK)
                    pieces = (g[c : c + CHUNK], g, NT) if side == 0 else (gt[c : c + CHUNK], g, NN)
                    high, low = split(0.95 * gram[s, rows, :] + 0.05 * dot(*pieces))
                    a_high[m, rows, :] = high
                    a_low[m, rows, :] = low

        def sweep(carry):
            phase, limit = carry

            @pl.when(phase < 2)
            def _():
                @pl.loop(0, SLOTS)
                def _(s):
                    z[SLOTS * s] = left[s].T
                    z[SLOTS * s + 1] = right[s].T

            worst_ref[...] = jnp.zeros((1, 128), f32)

            @pl.loop(0, MATS)
            def _(m):
                @pl.when(wanted[m // SLOTS] != 0)
                def _():
                    @pl.loop(0, jnp.where(phase == 0, 2, 1))
                    def _(_):
                        for c in range(0, BLOCK, CHUNK):
                            rows = pl.ds(c, CHUNK)
                            z[m, rows, :] = unit_rows(dot3(split(z[m, rows, :]), (a_high[m], a_low[m])))

            orthonormal_rows(z, work, worst_ref)
            slot = lax.broadcasted_iota(jnp.int32, (1, 128), 1) // (128 // SLOTS)
            counts = (slot == 0) & (wanted[0] != 0) | (slot == 1) & (wanted[1] != 0)
            bad = jnp.max(jnp.where(counts, worst_ref[...], 0.0)) > 0.5
            return phase + 1, jnp.where((phase == 0) & bad, 3, limit)

        lax.while_loop(lambda carry: carry[0] < carry[1], sweep, (jnp.int32(0), jnp.int32(1)))

        @pl.loop(0, SLOTS)
        def _(s):
            @pl.when(wanted[s] != 0)
            def _():
                new_left[s] = z[SLOTS * s].T
                new_right[s] = z[SLOTS * s + 1].T


def pack_kernel(table, gradient, outbox):
    @pl.loop(0, outbox.shape[0])
    def _(k):
        start = pl.multiple_of(jnp.maximum(table[k], 0) * BLOCK, BLOCK)
        piece = gradient[:, pl.ds(start, BLOCK)]
        outbox[k] = jnp.where(table[k] >= 0, piece, jnp.zeros_like(piece))


def step(held, wanted, grads, first, second, left_gram, right_gram, left, right):
    vmem = pl.BlockSpec(memory_space=pltpu.VMEM)
    smem = pl.BlockSpec(memory_space=pltpu.SMEM)
    whole = jax.ShapeDtypeStruct((SLOTS, BLOCK, BLOCK), f32)
    return pl.pallas_call(
        step_kernel,
        out_shape=(whole, whole, whole),
        in_specs=[smem, smem] + [vmem] * 7,
        out_specs=(vmem, vmem, vmem),
        scratch_shapes=[
            pltpu.VMEM((MATS, BLOCK, BLOCK), f32),
            pltpu.VMEM((MATS, BLOCK, BLOCK), bf16),
            pltpu.VMEM((MATS, BLOCK, BLOCK), bf16),
            pltpu.VMEM((MATS, PANEL, PANEL), f32),
            pltpu.VMEM((1, 128), f32),
            pltpu.VMEM((BLOCK, BLOCK), f32),
        ],
        compiler_params=pltpu.CompilerParams(vmem_limit_bytes=56 * 1024 * 1024),
    )(held, wanted, grads, first, second, left_gram, right_gram, left, right)


def local(
    gradient, slot_block, refresh_target, first_moment, second_moment, left_gram, right_gram, left_basis, right_basis
):
    owners = lax.axis_size("dp")
    owner = lax.axis_index("dp")
    device = owner * lax.axis_size("tensor") + lax.axis_index("tensor")
    table = slot_block[0]
    slab = gradient.shape[2]
    vmem = pl.BlockSpec(memory_space=pltpu.VMEM)
    smem = pl.BlockSpec(memory_space=pltpu.SMEM)
    outbox = pl.pallas_call(
        pack_kernel,
        out_shape=jax.ShapeDtypeStruct((owners * SLOTS, slab, BLOCK), bf16),
        in_specs=[smem, vmem],
        out_specs=vmem,
    )(table, gradient[0, 0])
    grads = lax.all_to_all(outbox.reshape(owners, SLOTS, slab, BLOCK), "dp", 0, 0, tiled=True)
    held = (lax.dynamic_slice_in_dim(table, owner * SLOTS, SLOTS) >= 0).astype(jnp.int32)
    wanted = (lax.dynamic_slice_in_dim(refresh_target, device * SLOTS, SLOTS) >= 0).astype(jnp.int32)
    outputs = step(
        held, wanted, grads, first_moment[0], second_moment[0], left_gram[0], right_gram[0], left_basis[0], right_basis[0]
    )
    return tuple(x[None] for x in outputs)


def solution(mesh):
    rows = P("tensor", "dp", None, None)
    return jax.shard_map(
        local,
        mesh=mesh,
        in_specs=(P("tensor", None, "dp", None), P("tensor", None), P(), rows, rows, rows, rows, rows, rows),
        out_specs=(rows, rows, rows),
        check_vma=False,
    )
```

time: 1020 us -> 130 us (0.13); the launches traced: 1010 us -> 128 us
  other arithmetic: 542 us -> 1.25 us
  waiting for transfers between devices: 225 us -> 15.6 us
  local copies, waits for them, and re-layouts: 110 us -> 0.98 us
  Pallas kernels: 0 us -> 100 us
  matrix products: 89.9 us -> 0 us
  starting transfers between devices: 37.4 us -> 8.77 us
    another operation x39 -> x0, other arithmetic: 508 us -> none  [the longest x32 338 us: orthonormal(): factor = jnp.linalg.cholesky(inner)]
    all_to_all x5 -> x1, waiting for transfers between devices: 225 us -> 15.6 us  [local(): lax.all_to_all(outbox.reshape(owners, SLOTS, slab, BLOCK), 'dp', 0, 0, ti...]
    pallas_call x0 -> x2, Pallas kernels: none -> 100 us  [the longest x1 97.6 us: step(): pl.pallas_call(step_kernel, out_shape=(whole, whole, whole), in_specs=[sm...]
    another operation x42 -> x0, local copies, waits for them, and re-layouts: 53 us -> none  [the longest x28 34.6 us: orthonormal(): lax.linalg.triangular_solve(factor, image, left_side=False, lower=True, t...]
    another operation x26 -> x0, matrix products: 49.2 us -> none  [the longest x14 25.4 us: orthonormal(): lax.linalg.triangular_solve(factor, image, left_side=False, lower=True, t...]
    dot_general x10 -> x0, matrix products: 40.7 us -> none  [the longest x2 10.2 us: orthonormal(): inner = jnp.einsum('bki,bkj->bij', image, image, precision=highest)]
    all_to_all x5 -> x1, starting transfers between devices: 37.4 us -> 8.77 us  [local(): lax.all_to_all(outbox.reshape(owners, SLOTS, slab, BLOCK), 'dp', 0, 0, ti...]
    select_n x5 -> x0, other arithmetic: 18.3 us -> none  [the longest x1 6.05 us: local(): new_right = jnp.where(wanted[:, None, None], fresh_right, right_old)]
  transfers between devices with their start and end apart: 5 -> 1, of which waited for: 5 -> 1; matrix products, arithmetic and copies ran while one was open for 2% -> 1% of each run, Pallas kernels for 0% -> 0%
where the time goes in v1:
time: 130 us; the launch traced here: 128 us
  Pallas kernels  100 us (77%)
  waiting for transfers between devices  15.6 us (12%)
  starting transfers between devices  8.77 us (7%)
    pallas_call x1, Pallas kernels, step(): pl.pallas_call(step_kernel, out_shape=(whole, whole, whole), in_specs=[sm...  97.6 us
    all_to_all x1, waiting for transfers between devices, local(): lax.all_to_all(outbox.reshape(owners, SLOTS, slab, BLOCK), 'dp', 0, 0, ti...  15.6 us
    all_to_all x1, starting transfers between devices, local(): lax.all_to_all(outbox.reshape(owners, SLOTS, slab, BLOCK), 'dp', 0, 0, ti...  8.77 us
    pallas_call x1, Pallas kernels, local(): pl.pallas_call(pack_kernel, out_shape=jax.ShapeDtypeStruct((owners * SLOT...  2.64 us
  transfers between devices with their start and end apart: 1, of which 1 were waited for; matrix products, arithmetic and copies ran while one was open for 1% of the time, Pallas kernels for 0%

profile of v1, /device:TPU:3, one launch (start us, length us, event | category | flops | bytes accessed | tf_op | source)
XLA Modules:
  0.0 127.6 jit_solution(11606930731884307618)
XLA Ops:
  0.6 0.0 copy-start.1
  0.6 0.0 copy-start.2
  0.7 2.6 %shard_map.112 = bf16[64,16,512]{2,1,0:T(8,128)(2,1)} custom-call(s32[64]{0:T(128)} %bitcast.22, bf16[16,16384]{1,0:T(8,128)(2,1)} %bitcast.21), custom_call_target="tpu_custom_call" | custom-call | tf_op jit(solution)/shard_map/pallas_call | solution.py:245
  3.3 8.8 %all-to-all-start = ((bf16[32,2,16,512]{3,2,1,0:T(8,128)(2,1)}), bf16[32,2,16,512]{3,2,1,0:T(8,128)(2,1)S(1)}, u32[]{:S(2)}, u32[]{:S(2)}) async-start(bf16[32,2,16,512]{3,2,1,0:T(8,128)(2,1)} %bitcast.14), calls=%async_computation | async-start | bytes 2097152 | tf_op jit(solution)/shard_map/all_to_all | solution.py:251
  12.1 0.0 copy-done.1
  12.1 0.6 fusion.held
  12.7 0.0 copy-done.2
  12.7 0.6 compare_convert_fusion.wanted
  13.3 15.6 %all-to-all-done.grads = bf16[32,2,16,512]{3,2,1,0:T(8,128)(2,1)S(1)} async-done(((bf16[32,2,16,512]{3,2,1,0:T(8,128)(2,1)}), bf16[32,2,16,512]{3,2,1,0:T(8,128)(2,1)S(1)}, u32[]{:S(2)}, u32[]{:S(2)}) %all-to-all-start) | async-done | bytes 1048608 | tf_op jit(solution)/shard_map/all_to_all | solution.py:251
  29.0 0.0 copy-start
  29.0 1.0 copy-done
  30.0 97.6 %shard_map.113 = (f32[2,512,512]{2,1,0:T(8,128)}, f32[2,512,512]{2,1,0:T(8,128)}, f32[2,512,512]{2,1,0:T(8,128)}) custom-call(s32[2]{0:T(128)} %fusion.held, s32[2]{0:T(128)} %compare_convert_fusion.wanted, bf16[32,2,16,512]{3,2,1,0:T(8,128)(2,1)} %copy-done, f32[2,512,512]{2,1,0:T(8,128)} %bitcast.15, f32[2,512,512]{2,1,0:T(8,128)} %bitcast.16, ...), custom_call_target="tpu_custom_call" | custom-call | tf_op jit(solution)/shard_map/pallas_call | solution.py:218
Async XLA Ops:
  0.6 11.4 %copy-start.1 = (s32[1,64]{1,0:T(1,128)S(1)}, s32[1,64]{1,0:T(1,128)}, u32[]{:S(2)}) copy-start(s32[1,64]{1,0:T(1,128)} %param.10) | copy-start | bytes 772
  0.6 12.1 %copy-start.2 = (s32[256]{0:T(256)S(1)}, s32[256]{0:T(256)}, u32[]{:S(2)}) copy-start(s32[256]{0:T(256)} %param.11) | copy-start | bytes 3076
  3.3 25.7 %all-to-all-start = ((bf16[32,2,16,512]{3,2,1,0:T(8,128)(2,1)}), bf16[32,2,16,512]{3,2,1,0:T(8,128)(2,1)S(1)}, u32[]{:S(2)}, u32[]{:S(2)}) async-start(bf16[32,2,16,512]{3,2,1,0:T(8,128)(2,1)} %bitcast.14), calls=%async_computation | async-start | bytes 2097152 | tf_op jit(solution)/shard_map/all_to_all | solution.py:251
  29.0 1.0 copy-start

commit v2 on v1

v2 whole, which is shorter than its diff:
```python
import functools

import jax
import jax.numpy as jnp
from jax import lax
from jax.experimental import pallas as pl
from jax.experimental.pallas import tpu as pltpu
from jax.sharding import PartitionSpec as P

BLOCK = 512
PANEL = 256
SUB = 128
LEAF = 32
SLOTS = 2
MATS = 2 * SLOTS
CHUNK = 256
WORST = 17.0

f32 = jnp.float32
bf16 = jnp.bfloat16

NN = (((1,), (0,)), ((), ()))
NT = (((1,), (1,)), ((), ()))
TN = (((0,), (0,)), ((), ()))


def split(x):
    high = x.astype(bf16)
    return high, (x - high.astype(f32)).astype(bf16)


def dot(a, b, dims=NN):
    return lax.dot_general(a, b, dims, preferred_element_type=f32)


def dot3(a, b, dims=NN):
    return dot(a[0], b[0], dims) + (dot(a[0], b[1], dims) + dot(a[1], b[0], dims))


def unit_rows(x):
    return x * lax.rsqrt(jnp.sum(x * x, axis=1, keepdims=True))


def leaf(tiles):
    lane = lax.broadcasted_iota(jnp.int32, (8, 128), 1)
    row = lax.broadcasted_iota(jnp.int32, (8, 128), 0)
    within = lane % LEAF
    base = lane - within
    worst = jnp.zeros((1, 128), f32)
    tiles = list(tiles)
    depth = LEAF // 8
    pick = lambda t, j: jnp.take_along_axis(tiles[t], base + j, axis=1)
    columns = [[pick(t, q) for t in range(depth)] for q in range(8)]
    for t0 in range(depth):
        ahead = [[pick(t, 8 * t0 + 8 + q) for t in range(t0 + 1, depth)] for q in range(8)] if t0 + 1 < depth else []
        for q in range(8):
            inverse = lax.rsqrt(columns[q][0][q : q + 1, :])
            worst = jnp.maximum(worst, jnp.where(inverse < WORST, 0.0, 1.0))
            factors = [column * inverse for column in columns[q]]
            factors[0] = jnp.where(row > q, factors[0], 0.0)
            for r in range(q + 1, 8):
                across = factors[0][r : r + 1, :]
                columns[r] = [column - factor * across for column, factor in zip(columns[r], factors)]
            here = within[:1] == 8 * t0 + q
            scaled = (tiles[t0][q : q + 1, :] + jnp.where(here, 1.0, 0.0)) * inverse
            for t in range(t0, depth):
                tiles[t] = tiles[t] - factors[t - t0] * scaled
            tiles[t0] = jnp.where(row == q, jnp.where(here, inverse, scaled), tiles[t0])
            for r in range(8 if ahead else 0):
                across = factors[1][r : r + 1, :]
                ahead[r] = [column - factor * across for column, factor in zip(ahead[r], factors[1:])]
        columns = ahead
    for t in range(LEAF // 8):
        tiles[t] = jnp.where(within <= row + 8 * t, tiles[t], 0.0)
    return tiles, worst


def rotated(x, m):
    cut = SUB - m * LEAF
    return x if m == 0 else jnp.concatenate([x[cut:], x[:cut]], axis=0)


def factor(work, worst_ref, tasks):
    lane = lax.broadcasted_iota(jnp.int32, (SUB, SUB), 1)
    row = lax.broadcasted_iota(jnp.int32, (SUB, SUB), 0)
    group = lane // LEAF
    own = group == row // LEAF
    for b in range(SUB // LEAF):
        top = b * LEAF
        rows = slice(top, top + LEAF)
        stacked = jnp.concatenate([work[(g - b) % MATS, rows, :] for g in range(MATS)], axis=0)
        packed = stacked[:LEAF]
        for g in range(1, MATS):
            packed = jnp.where(group[:LEAF] == g, stacked[g * LEAF : (g + 1) * LEAF], packed)
        tiles, worst = leaf([packed[8 * t : 8 * t + 8] for t in range(LEAF // 8)])
        tasks[b]()
        worst_ref[...] = jnp.maximum(worst_ref[...], worst)
        inverse = jnp.where(own, jnp.concatenate(tiles * MATS, axis=0), 0.0)
        pair = split(inverse)
        band = jnp.where(own, inverse, dot3(pair, split(stacked)))
        height = SUB - top - LEAF
        if height:
            under = slice(top + LEAF, SUB)
            old = jnp.concatenate([work[m, under, :] for m in range(MATS)], axis=0)
            mine = jnp.concatenate([group[:height] == (b + m) % MATS for m in range(MATS)], axis=0)
            factors = jnp.where(mine, dot3(split(old), pair, NT), 0.0)
            fresh = jnp.where(mine, 0.0, old) - dot3(split(factors), split(band))
            for m in range(MATS):
                work[m, under, :] = fresh[m * height : (m + 1) * height]
        for g in range(MATS):
            work[(g - b) % MATS, rows, :] = band[g * LEAF : (g + 1) * LEAF]
    for m in range(MATS):
        column = (lane + (SUB - m * LEAF)) % SUB
        work[m] = jnp.where(column <= row, work[m], 0.0)


def orthonormal_rows(z, work, low, turned_high, turned_low, worst_ref, wanted, tasks):
    lane = lax.broadcasted_iota(jnp.int32, (SUB, SUB), 1)
    row = lax.broadcasted_iota(jnp.int32, (SUB, SUB), 0)

    def guarded(m, x):
        unit = jnp.where((lane + (SUB - m * LEAF)) % SUB == row, 1.0, 0.0)
        return jnp.where(wanted[m // SLOTS] != 0, x, unit)

    for p in range(BLOCK // PANEL):
        here = slice(p * PANEL, (p + 1) * PANEL)
        for m in range(MATS):
            part = split(z[m, here, :])
            turned = tuple(jnp.concatenate([rotated(x[:SUB], m), rotated(x[SUB:], m)], axis=0) for x in part)
            turned_high[m] = turned[0]
            turned_low[m] = turned[1]
            product = dot3(part, turned, NT)
            work[m] = guarded(m, product[:SUB, :SUB])
            low[m] = product[SUB:, :SUB]
            z[m, PANEL * p + SUB : PANEL * (p + 1), :SUB] = product[SUB:, SUB:]
        factor(work, worst_ref, tasks[8 * p : 8 * p + 4])
        for m in range(MATS):
            inverse = split(work[m])
            across = split(dot3(split(low[m]), inverse, NT))
            gram_m = z[m, PANEL * p + SUB : PANEL * (p + 1), :SUB]
            low[m] = dot3(across, inverse)
            z[m, PANEL * p : PANEL * p + SUB, :SUB] = work[m]
            work[m] = guarded(m, gram_m - dot3(across, tuple(rotated(x, m) for x in across), NT))
        factor(work, worst_ref, tasks[8 * p + 4 : 8 * p + 8])
        for m in range(MATS):
            lower = split(work[m])
            cross = dot3(lower, tuple(rotated(x, m) for x in split(low[m])))
            upper = z[m, PANEL * p : PANEL * p + SUB, :SUB]
            whole = jnp.concatenate(
                [
                    jnp.concatenate([upper, jnp.zeros((SUB, SUB), f32)], axis=1),
                    jnp.concatenate([-cross, work[m]], axis=1),
                ],
                axis=0,
            )
            fresh = dot3(split(whole), (turned_high[m], turned_low[m]))
            z[m, here, :] = fresh
            if p + 1 < BLOCK // PANEL:
                rest = slice((p + 1) * PANEL, BLOCK)
                fresh = split(fresh)
                old = z[m, rest, :]
                along = dot3(split(old), fresh, NT)
                z[m, rest, :] = old - dot3(split(along), fresh)


def step_kernel(
    held, wanted, grads, first_in, second_in, left_gram_in, right_gram_in, left_in, right_in,
    update_out, new_left, new_right,
    g, first, second, left_gram, right_gram, left, right, update, left_high, left_low, temp,
    z, a_high, a_low, work, low, turned_high, turned_low, worst_ref, in_sems, out_sems,
):
    grams = (left_gram, right_gram)
    halves = [slice(c, c + CHUNK) for c in range(0, BLOCK, CHUNK)]
    g_copies = [pltpu.make_async_copy(grads.at[:, s], g.at[s], in_sems.at[s]) for s in range(SLOTS)]
    left_copy, right_copy, left_gram_copy, right_gram_copy, first_copy, second_copy = [
        pltpu.make_async_copy(source, target, in_sems.at[SLOTS + i])
        for i, (source, target) in enumerate(
            (
                (left_in, left),
                (right_in, right),
                (left_gram_in, left_gram),
                (right_gram_in, right_gram),
                (first_in, first),
                (second_in, second),
            )
        )
    ]
    left_copy.start()
    right_copy.start()
    for copy in g_copies:
        copy.start()
    left_gram_copy.start()
    right_gram_copy.start()
    first_copy.start()
    second_copy.start()

    def g_block(s):
        return g[s].reshape(BLOCK, BLOCK)

    def first_product(s, rows):
        temp[s, rows, :] = dot(left_high[s, rows, :], g_block(s)) + dot(left_low[s, rows, :], g_block(s))

    def moments(s, rows):
        rotated_rows = dot3(split(temp[s, rows, :]), split(right[s]))
        moment = 0.9 * first[s, rows, :] + 0.1 * rotated_rows
        spread = 0.95 * second[s, rows, :] + 0.05 * rotated_rows * rotated_rows
        temp[s, rows, :] = moment / (jnp.sqrt(spread) + 1e-08)

    def back(s, rows):
        update[s, rows, :] = dot3(split(left[s, rows, :]), split(temp[s]))

    def finish(s, rows):
        result = dot3(split(update[s, rows, :]), split(right[s]), NT)
        update[s, rows, :] = jnp.where(held[s] != 0, result, 0.0)

    refresh = (wanted[0] + wanted[1]) != 0
    left_copy.wait()
    right_copy.wait()

    @pl.when((held[0] + held[1]) != 0)
    def _():
        for s in range(SLOTS):
            high, low_part = split(left[s].T)
            left_high[s] = high
            left_low[s] = low_part

    for copy in g_copies:
        copy.wait()
    left_gram_copy.wait()
    right_gram_copy.wait()
    first_copy.wait()
    second_copy.wait()

    @pl.when(jnp.logical_not(refresh))
    def _():
        @pl.loop(0, SLOTS)
        def _(s):
            @pl.when(held[s] == 0)
            def _():
                update[s] = jnp.zeros((BLOCK, BLOCK), f32)

            @pl.when(held[s] != 0)
            def _():
                for stage in (first_product, moments, back, finish):
                    for rows in halves:
                        stage(s, rows)

    @pl.when(refresh)
    def _():
        @pl.loop(0, SLOTS)
        def _(s):
            gs = g_block(s)
            gt = gs.T
            for side in range(2):
                m = SLOTS * s + side
                for rows in halves:
                    pieces = (gs[rows], gs, NT) if side == 0 else (gt[rows], gs, NN)
                    high, low_part = split(0.95 * grams[side][s, rows, :] + 0.05 * dot(*pieces))
                    a_high[m, rows, :] = high
                    a_low[m, rows, :] = low_part

        def turn_back(m, columns):
            grams[m % 2][m // 2, :, columns] = z[m, columns, :].T

        tasks = []
        for stage in (first_product, moments, back, finish):
            for s in range(SLOTS):
                for rows in halves:
                    tasks.append(functools.partial(stage, s, rows))
        for m in range(MATS):
            tasks[8 + 2 * m] = functools.partial(
                lambda m, task: (task(), turn_back(m, slice(0, PANEL))), m, tasks[8 + 2 * m]
            )

        def sweep(carry):
            phase, limit = carry

            @pl.when(phase < 2)
            def _():
                @pl.loop(0, SLOTS)
                def _(s):
                    z[SLOTS * s] = left[s].T
                    z[SLOTS * s + 1] = right[s].T

            worst_ref[...] = jnp.zeros((1, 128), f32)

            @pl.loop(0, MATS)
            def _(m):
                @pl.when(wanted[m // SLOTS] != 0)
                def _():
                    @pl.loop(0, jnp.where(phase == 0, 2, 1))
                    def _(_):
                        for rows in halves:
                            z[m, rows, :] = unit_rows(dot3(split(z[m, rows, :]), (a_high[m], a_low[m])))

            orthonormal_rows(z, work, low, turned_high, turned_low, worst_ref, wanted, tasks)
            bad = jnp.max(worst_ref[...]) > 0.5
            return phase + 1, jnp.where((phase == 0) & bad, 3, limit)

        lax.while_loop(lambda carry: carry[0] < carry[1], sweep, (jnp.int32(0), jnp.int32(1)))

    update_copy = pltpu.make_async_copy(update, update_out, out_sems.at[0])
    update_copy.start()
    for m in range(MATS):
        s, side = divmod(m, 2)
        target = (new_left, new_right)[side].at[s]
        semaphore = out_sems.at[1 + m]

        @pl.when(wanted[s] != 0)
        def _():
            grams[side][s, :, PANEL:] = z[m, PANEL:, :].T
            pltpu.make_async_copy(grams[side].at[s], target, semaphore).start()

        @pl.when(wanted[s] == 0)
        def _():
            pltpu.make_async_copy((left, right)[side].at[s], target, semaphore).start()

    update_copy.wait()
    for m in range(MATS):
        s, side = divmod(m, 2)
        pltpu.make_async_copy(grams[side].at[s], (new_left, new_right)[side].at[s], out_sems.at[1 + m]).wait()


def pack_kernel(table, gradient, outbox):
    @pl.loop(0, outbox.shape[0])
    def _(k):
        start = pl.multiple_of(jnp.maximum(table[k], 0) * BLOCK, BLOCK)
        piece = gradient[:, pl.ds(start, BLOCK)]
        outbox[k] = jnp.where(table[k] >= 0, piece, jnp.zeros_like(piece))


def step(held, wanted, grads, first, second, left_gram, right_gram, left, right):
    anywhere = pl.BlockSpec(memory_space=pl.ANY)
    smem = pl.BlockSpec(memory_space=pltpu.SMEM)
    whole = jax.ShapeDtypeStruct((SLOTS, BLOCK, BLOCK), f32)
    return pl.pallas_call(
        step_kernel,
        out_shape=(whole, whole, whole),
        in_specs=[smem, smem] + [anywhere] * 7,
        out_specs=(anywhere, anywhere, anywhere),
        scratch_shapes=[pltpu.VMEM((SLOTS, *grads.shape[:1], *grads.shape[2:]), bf16)]
        + [pltpu.VMEM((SLOTS, BLOCK, BLOCK), f32)] * 7
        + [pltpu.VMEM((SLOTS, BLOCK, BLOCK), bf16)] * 2
        + [
            pltpu.VMEM((SLOTS, BLOCK, BLOCK), f32),
            pltpu.VMEM((MATS, BLOCK, BLOCK), f32),
            pltpu.VMEM((MATS, BLOCK, BLOCK), bf16),
            pltpu.VMEM((MATS, BLOCK, BLOCK), bf16),
            pltpu.VMEM((MATS, SUB, SUB), f32),
            pltpu.VMEM((MATS, SUB, SUB), f32),
            pltpu.VMEM((MATS, PANEL, BLOCK), bf16),
            pltpu.VMEM((MATS, PANEL, BLOCK), bf16),
            pltpu.VMEM((1, 128), f32),
            pltpu.SemaphoreType.DMA((SLOTS + 6,)),
            pltpu.SemaphoreType.DMA((1 + MATS,)),
        ],
        compiler_params=pltpu.CompilerParams(vmem_limit_bytes=48 * 1024 * 1024),
    )(held, wanted, grads, first, second, left_gram, right_gram, left, right)


def local(
    gradient, slot_block, refresh_target, first_moment, second_moment, left_gram, right_gram, left_basis, right_basis
):
    owners = lax.axis_size("dp")
    owner = lax.axis_index("dp")
    device = owner * lax.axis_size("tensor") + lax.axis_index("tensor")
    table = slot_block[0]
    slab = gradient.shape[2]
    vmem = pl.BlockSpec(memory_space=pltpu.VMEM)
    smem = pl.BlockSpec(memory_space=pltpu.SMEM)
    outbox = pl.pallas_call(
        pack_kernel,
        out_shape=jax.ShapeDtypeStruct((owners * SLOTS, slab, BLOCK), bf16),
        in_specs=[smem, vmem],
        out_specs=vmem,
    )(table, gradient[0, 0])
    grads = lax.all_to_all(outbox.reshape(owners, SLOTS, slab, BLOCK), "dp", 0, 0, tiled=True)
    held = (lax.dynamic_slice_in_dim(table, owner * SLOTS, SLOTS) >= 0).astype(jnp.int32)
    wanted = (lax.dynamic_slice_in_dim(refresh_target, device * SLOTS, SLOTS) >= 0).astype(jnp.int32)
    outputs = step(
        held, wanted, grads, first_moment[0], second_moment[0], left_gram[0], right_gram[0], left_basis[0], right_basis[0]
    )
    return tuple(x[None] for x in outputs)


def solution(mesh):
    rows = P("tensor", "dp", None, None)
    return jax.shard_map(
        local,
        mesh=mesh,
        in_specs=(P("tensor", None, "dp", None), P("tensor", None), P(), rows, rows, rows, rows, rows, rows),
        out_specs=(rows, rows, rows),
        check_vma=False,
    )
```

time: 130 us -> 72.8 us (0.56)
  the two profiles are of different devices: /device:TPU:3 before, /device:TPU:5 now
where the time goes in v2:
time: 72.8 us; the launch traced here: 71.4 us
  Pallas kernels  43.3 us (59%)
  waiting for transfers between devices  16.7 us (23%)
  starting transfers between devices  8.77 us (12%)
  local copies, waits for them, and re-layouts  1.6 us (2%)
  between operations  0.86 us (1%)
    pallas_call x1, Pallas kernels, step(): pl.pallas_call(step_kernel, out_shape=(whole, whole, whole), in_specs=[sm...  40.5 us
    all_to_all x1, waiting for transfers between devices, local(): lax.all_to_all(outbox.reshape(owners, SLOTS, slab, BLOCK), 'dp', 0, 0, ti...  16.7 us
    all_to_all x1, starting transfers between devices, local(): lax.all_to_all(outbox.reshape(owners, SLOTS, slab, BLOCK), 'dp', 0, 0, ti...  8.77 us
    pallas_call x1, Pallas kernels, local(): pl.pallas_call(pack_kernel, out_shape=jax.ShapeDtypeStruct((owners * SLOT...  2.78 us
    unnamed x8, local copies, waits for them, and re-layouts  1.6 us
  transfers between devices with their start and end apart: 1, of which 1 were waited for; matrix products, arithmetic and copies ran while one was open for 0% of the time, Pallas kernels for 0%

profile of v2, /device:TPU:5, one launch (start us, length us, event | category | flops | bytes accessed | tf_op | source)
XLA Modules:
  0.0 71.4 jit_solution(12249106132592997743)
XLA Ops:
  0.6 0.0 copy-start.2
  0.6 0.0 copy-start.3
  0.7 0.0 copy-start
  0.7 2.8 %shard_map.112 = bf16[64,16,512]{2,1,0:T(8,128)(2,1)} custom-call(s32[64]{0:T(128)} %bitcast.22, bf16[16,16384]{1,0:T(8,128)(2,1)} %bitcast.21), custom_call_target="tpu_custom_call" | custom-call | tf_op jit(solution)/shard_map/pallas_call | solution.py:371
  3.4 8.8 %all-to-all-start = ((bf16[32,2,16,512]{3,2,1,0:T(8,128)(2,1)}), bf16[32,2,16,512]{3,2,1,0:T(8,128)(2,1)S(1)}, u32[]{:S(2)}, u32[]{:S(2)}) async-start(bf16[32,2,16,512]{3,2,1,0:T(8,128)(2,1)} %bitcast.16), calls=%async_computation | async-start | bytes 2097152 | tf_op jit(solution)/shard_map/all_to_all | solution.py:377
  12.2 0.0 copy-done.2
  12.2 0.1 fusion.held
  12.3 0.0 copy-done.3
  12.3 0.1 compare_convert_fusion.wanted
  12.4 16.7 %all-to-all-done.grads = bf16[32,2,16,512]{3,2,1,0:T(8,128)(2,1)S(1)} async-done(((bf16[32,2,16,512]{3,2,1,0:T(8,128)(2,1)}), bf16[32,2,16,512]{3,2,1,0:T(8,128)(2,1)S(1)}, u32[]{:S(2)}, u32[]{:S(2)}) %all-to-all-start) | async-done | bytes 1048608 | tf_op jit(solution)/shard_map/all_to_all | solution.py:377
  29.1 0.0 copy-done
  29.1 0.0 copy-start.1
  29.1 1.6 %copy-done.1 = f32[1,2,512,512]{3,2,1,0:T(8,128)S(1)} copy-done((f32[1,2,512,512]{3,2,1,0:T(8,128)S(1)}, f32[1,2,512,512]{3,2,1,0:T(8,128)}, u32[]{:S(2)}) %copy-start.1) | copy-done | bytes 2097176
  30.7 40.5 %shard_map.113 = (f32[2,512,512]{2,1,0:T(8,128)}, f32[2,512,512]{2,1,0:T(8,128)}, f32[2,512,512]{2,1,0:T(8,128)}) custom-call(s32[2]{0:T(128)S(1)} %fusion.held, s32[2]{0:T(128)S(1)} %compare_convert_fusion.wanted, bf16[32,2,16,512]{3,2,1,0:T(8,128)(2,1)S(1)} %all-to-all-done.grads, f32[2,512,512]{2,1,0:T(8,128)S(1)} %bitcast.14, ...), custom_call_target="tpu_custom_call" | custom-call | tf_op jit(solution)/shard_map/pallas_call | solution.py:336
Async XLA Ops:
  0.6 11.6 %copy-start.2 = (s32[1,64]{1,0:T(1,128)S(1)}, s32[1,64]{1,0:T(1,128)}, u32[]{:S(2)}) copy-start(s32[1,64]{1,0:T(1,128)} %param.10) | copy-start | bytes 772
  0.6 11.7 %copy-start.3 = (s32[256]{0:T(256)S(1)}, s32[256]{0:T(256)}, u32[]{:S(2)}) copy-start(s32[256]{0:T(256)} %param.11) | copy-start | bytes 3076
  0.7 28.5 %copy-start = (f32[1,2,512,512]{3,2,1,0:T(8,128)S(1)}, f32[1,2,512,512]{3,2,1,0:T(8,128)}, u32[]{:S(2)}) copy-start(f32[1,2,512,512]{3,2,1,0:T(8,128)} %param.12) | copy-start | bytes 6291460
  3.4 25.7 %all-to-all-start = ((bf16[32,2,16,512]{3,2,1,0:T(8,128)(2,1)}), bf16[32,2,16,512]{3,2,1,0:T(8,128)(2,1)S(1)}, u32[]{:S(2)}, u32[]{:S(2)}) async-start(bf16[32,2,16,512]{3,2,1,0:T(8,128)(2,1)} %bitcast.16), calls=%async_computation | async-start | bytes 2097152 | tf_op jit(solution)/shard_map/all_to_all | solution.py:377
  29.1 1.6 %copy-start.1 = (f32[1,2,512,512]{3,2,1,0:T(8,128)S(1)}, f32[1,2,512,512]{3,2,1,0:T(8,128)}, u32[]{:S(2)}) copy-start(f32[1,2,512,512]{3,2,1,0:T(8,128)} %param.13) | copy-start | bytes 6291460

commit v3 on v2

v3 whole, which is shorter than its diff:
```python
import functools

import jax
import jax.numpy as jnp
from jax import lax
from jax.experimental import pallas as pl
from jax.experimental.pallas import tpu as pltpu
from jax.sharding import PartitionSpec as P

BLOCK = 512
SUB = 128
LEAF = 32
SLOTS = 2
MATS = 2 * SLOTS
CHUNK = 256
WORST = 10.0
LEAF_WEIGHTS = [2, 2, 2, 2, 2, 2]

f32 = jnp.float32
bf16 = jnp.bfloat16

NN = (((1,), (0,)), ((), ()))
NT = (((1,), (1,)), ((), ()))
TN = (((0,), (0,)), ((), ()))


def split(x):
    high = x.astype(bf16)
    return high, (x - high.astype(f32)).astype(bf16)


def dot(a, b, dims=NN):
    return lax.dot_general(a, b, dims, preferred_element_type=f32)


def dot3(a, b, dims=NN):
    return dot(a[0], b[0], dims) + (dot(a[0], b[1], dims) + dot(a[1], b[0], dims))


def dot3_tile(a, b, dims=NN):
    zeros = jnp.zeros((SUB, SUB), bf16)
    if dims == NN:
        top, bottom = (b[0], b[1]), (b[0], zeros)
    else:
        top, bottom = (b[0], b[0]), (b[1], zeros)
    operand = jnp.concatenate([jnp.concatenate(top, axis=1), jnp.concatenate(bottom, axis=1)], axis=0)
    result = dot(jnp.concatenate(a, axis=1), operand, dims)
    return result[:, :SUB] + result[:, SUB:]


def dot3_deep(a, b):
    return dot(jnp.concatenate(a, axis=1), jnp.concatenate([b[0], b[0]], axis=0)) + dot(a[0], b[1])


def dot3_narrow(a, b):
    result = dot(a[0], jnp.concatenate(b, axis=0), NT)
    return result[:, :SUB] + (result[:, SUB:] + dot(a[1], b[0], NT))


def unit_rows(x):
    return x * lax.rsqrt(jnp.sum(x * x, axis=1, keepdims=True))


def leaf(tiles, hooks):
    lane = lax.broadcasted_iota(jnp.int32, (8, 128), 1)
    row = lax.broadcasted_iota(jnp.int32, (8, 128), 0)
    within = lane % LEAF
    base = lane - within
    worst = jnp.zeros((1, 128), f32)
    tiles = list(tiles)
    depth = LEAF // 8
    pick = lambda t, j: jnp.take_along_axis(tiles[t], base + j, axis=1)
    columns = [[pick(t, q) for t in range(depth)] for q in range(8)]
    for t0 in range(depth):
        ahead = [[pick(t, 8 * t0 + 8 + q) for t in range(t0 + 1, depth)] for q in range(8)] if t0 + 1 < depth else []
        for q in range(8):
            inverse = lax.rsqrt(columns[q][0][q : q + 1, :])
            worst = jnp.maximum(worst, jnp.where(inverse < WORST, 0.0, 1.0))
            factors = [column * inverse for column in columns[q]]
            factors[0] = jnp.where(row > q, factors[0], 0.0)
            for r in range(q + 1, 8):
                across = factors[0][r : r + 1, :]
                columns[r] = [column - factor * across for column, factor in zip(columns[r], factors)]
            here = within[:1] == 8 * t0 + q
            scaled = (tiles[t0][q : q + 1, :] + jnp.where(here, 1.0, 0.0)) * inverse
            for t in range(t0, depth):
                tiles[t] = tiles[t] - factors[t - t0] * scaled
            tiles[t0] = jnp.where(row == q, jnp.where(here, inverse, scaled), tiles[t0])
            for r in range(8 if ahead else 0):
                across = factors[1][r : r + 1, :]
                ahead[r] = [column - factor * across for column, factor in zip(ahead[r], factors[1:])]
        columns = ahead
        hooks[t0]()
    for t in range(LEAF // 8):
        tiles[t] = jnp.where(within <= row + 8 * t, tiles[t], 0.0)
    return tiles, worst


def rotated(x, m):
    cut = SUB - m * LEAF
    return x if m == 0 else jnp.concatenate([x[cut:], x[:cut]], axis=0)


def factor(work, worst_ref, tasks):
    lane = lax.broadcasted_iota(jnp.int32, (SUB, SUB), 1)
    row = lax.broadcasted_iota(jnp.int32, (SUB, SUB), 0)
    group = lane // LEAF
    own = group == row // LEAF
    steps = SUB // LEAF
    current = [work[m, :LEAF, :] for m in range(MATS)]
    for b in range(steps):
        rows = slice(b * LEAF, (b + 1) * LEAF)
        stacked = jnp.concatenate([current[(g - b) % MATS] for g in range(MATS)], axis=0)
        packed = stacked[:LEAF]
        for g in range(1, MATS):
            packed = jnp.where(group[:LEAF] == g, stacked[g * LEAF : (g + 1) * LEAF], packed)
        tiles, worst = leaf([packed[8 * t : 8 * t + 8] for t in range(LEAF // 8)], tasks[6 * b : 6 * b + 4])
        worst_ref[...] = jnp.maximum(worst_ref[...], worst)
        inverse = jnp.where(own, jnp.concatenate(tiles * MATS, axis=0), 0.0)
        pair = split(inverse)

        height = SUB - (b + 2) * LEAF
        if b + 1 < steps:
            following = slice((b + 1) * LEAF, (b + 2) * LEAF)
            pieces = [(m, following, LEAF) for m in range(MATS)]
            if height:
                pieces += [(m, slice((b + 2) * LEAF, SUB), height) for m in range(MATS)]
            old = jnp.concatenate([work[m, under, :] for m, under, _ in pieces], axis=0)
            mine = jnp.concatenate([group[:size] == (b + m) % MATS for m, _, size in pieces], axis=0)
            factors = jnp.where(mine, dot3_tile(split(old), pair, NT), 0.0)
        band = jnp.where(own, inverse, dot3_tile(pair, split(stacked)))
        tasks[6 * b + 4]()
        if b + 1 < steps:
            fresh = jnp.where(mine, 0.0, old) - dot3_tile(split(factors), split(band))
            current = [fresh[m * LEAF : (m + 1) * LEAF] for m in range(MATS)]
            for m in range(MATS if height else 0):
                start = MATS * LEAF + m * height
                work[m, (b + 2) * LEAF :, :] = fresh[start : start + height]
        tasks[6 * b + 5]()
        for g in range(MATS):
            work[(g - b) % MATS, rows, :] = band[g * LEAF : (g + 1) * LEAF]
    for m in range(MATS):
        column = (lane + (SUB - m * LEAF)) % SUB
        work[m] = jnp.where(column <= row, work[m], 0.0)


def spread_out(tasks, weights):
    total = sum(cost for cost, _ in tasks)
    edges = [total * sum(weights[: i + 1]) / sum(weights) for i in range(len(weights))]
    shares = [[] for _ in weights]
    done = 0.0
    at = 0
    for cost, call in tasks:
        while at + 1 < len(weights) and done + cost / 2 > edges[at]:
            at += 1
        shares[at].append(call)
        done += cost

    def run(calls):
        for call in calls:
            call()

    return [functools.partial(run, calls) for calls in shares]


def prepare_kernel(
    left_in, right_in, left_gram_in, right_gram_in, first_in, second_in,
    turned, left, right, right_high, right_low, left_gram, right_gram, first, second, sems,
):
    copies = [
        pltpu.make_async_copy(source, target, sems.at[i])
        for i, (source, target) in enumerate(
            (
                (left_in, left),
                (right_in, right),
                (left_gram_in, left_gram),
                (right_gram_in, right_gram),
                (first_in, first),
                (second_in, second),
            )
        )
    ]
    for copy in copies:
        copy.start()
    copies[0].wait()
    for s in range(SLOTS):
        turned[2 * s] = left[s].T
    copies[1].wait()
    for s in range(SLOTS):
        turned[2 * s + 1] = right[s].T
        right_high[s], right_low[s] = split(right[s])
    for copy in copies[2:]:
        copy.wait()


def step_kernel(
    held, wanted, grads, turned, left, right, right_high, right_low, left_gram, right_gram, first, second,
    update_out, new_left, new_right,
    g, update, temp, z, a_high, a_low, work, near, square, fresh, worst_ref, in_sems, out_sems,
):
    halves = [slice(c, c + CHUNK) for c in range(0, BLOCK, CHUNK)]
    blocks = [slice(c, c + SUB) for c in range(0, BLOCK, SUB)]
    g_copies = [pltpu.make_async_copy(grads.at[:, s], g.at[s], in_sems.at[s]) for s in range(SLOTS)]
    for copy in g_copies:
        copy.start()
    for copy in g_copies:
        copy.wait()

    def g_block(s):
        return g[s].reshape(BLOCK, BLOCK)

    def right_pair(s):
        return right_high[s], right_low[s]

    def first_product(s, rows):
        high, low = split(turned[2 * s, rows, :])
        temp[s, rows, :] = dot(high, g_block(s)) + dot(low, g_block(s))

    def moments(s, rows):
        rotated_rows = dot3(split(temp[s, rows, :]), right_pair(s))
        moment = 0.9 * first[s, rows, :] + 0.1 * rotated_rows
        spread = 0.95 * second[s, rows, :] + 0.05 * rotated_rows * rotated_rows
        temp[s, rows, :] = moment / (jnp.sqrt(spread) + 1e-08)

    def back(s, rows):
        update[s, rows, :] = dot3(split(left[s, rows, :]), split(temp[s]))

    def finish(s, rows):
        result = dot3(split(update[s, rows, :]), right_pair(s), NT)
        update[s, rows, :] = jnp.where(held[s] != 0, result, 0.0)

    refresh = (wanted[0] + wanted[1]) != 0

    @pl.when(jnp.logical_not(refresh))
    def _():
        @pl.loop(0, SLOTS)
        def _(s):
            @pl.when(held[s] == 0)
            def _():
                update[s] = jnp.zeros((BLOCK, BLOCK), f32)

            @pl.when(held[s] != 0)
            def _():
                for stage in (first_product, moments, back, finish):
                    for rows in halves:
                        stage(s, rows)

    @pl.when(refresh)
    def _():
        for s in range(SLOTS):
            gs = g_block(s)
            gt = gs.T
            for side in range(2):
                m = SLOTS * s + side
                for rows in halves:
                    pieces = (gs[rows], gs, NT) if side == 0 else (gt[rows], gs, NN)
                    past = (left_gram, right_gram)[side][s, rows, :]
                    a_high[m, rows, :], a_low[m, rows, :] = split(0.95 * past + 0.05 * dot(*pieces))

        def sweep(carry):
            phase, limit = carry
            worst_ref[...] = jnp.zeros((1, 128), f32)
            lane = lax.broadcasted_iota(jnp.int32, (SUB, SUB), 1)
            row = lax.broadcasted_iota(jnp.int32, (SUB, SUB), 0)

            def power(m, j):
                rows = blocks[j]
                source = jnp.where(phase == 2, z[m, rows, :], turned[m, rows, :])
                z[m, rows, :] = unit_rows(dot3(split(source), (a_high[m], a_low[m])))

            def again(m, j):
                rows = blocks[j]
                once = z[m, rows, :]
                z[m, rows, :] = jnp.where(phase == 0, unit_rows(dot3(split(once), (a_high[m], a_low[m]))), once)

            def products(m, j):
                part = split(z[m, blocks[j], :])
                other = [tuple(rotated(x, m) for x in part)]
                if j:
                    other.append(tuple(rotated(x, m) for x in split(z[m, blocks[j - 1], :])))
                result = dot3(part, tuple(jnp.concatenate(x, axis=0) for x in zip(*other)), NT) if j else dot3_narrow(part, other[0])
                square[m] = result[:, :SUB]
                if j:
                    near[m] = result[:, SUB:]

            def couple(m, j):
                value = dot3_tile(split(near[m]), split(inverses[j - 1][m]), NT)
                near[m] = value
                value = split(value)
                square[m] -= dot3_tile(value, tuple(rotated(x, m) for x in value), NT)

            def project(m, j):
                z[m, blocks[j], :] -= dot3_deep(split(near[m]), split(z[m, blocks[j - 1], :]))

            def align(m, j, count):
                fixed = split(z[m, : count * SUB, :])
                part = split(z[m, blocks[j], :])
                if count == 1:
                    z[m, blocks[j], :] -= dot3_deep(split(dot3_narrow(part, fixed)), fixed)
                else:
                    z[m, blocks[j], :] -= dot3(split(dot3(part, fixed, NT)), fixed)

            def scale(m, j):
                part = tuple(rotated(x, m) for x in split(z[m, blocks[j], :]))
                z[m, blocks[j], :] = dot3_deep(split(inverses[j][m]), part)

            def turn_back(m, columns):
                fresh[m, :, columns] = z[m, columns, :].T

            def guarded(m, x):
                unit = jnp.where((lane + (SUB - m * LEAF)) % SUB == row, 1.0, 0.0)
                return jnp.where(wanted[m // SLOTS] != 0, x, unit)

            def every(cost, task, *more):
                return [(cost, functools.partial(task, m, *more)) for m in range(MATS)]

            def step_tasks(cost, stage):
                return [(cost, functools.partial(stage, s, rows)) for s in range(SLOTS) for rows in blocks]

            inverses = [None] * len(blocks)
            firsts, middles, backs, ends = (
                step_tasks(cost, stage) for cost, stage in ((2, first_product), (3, moments), (3, back), (3, finish))
            )
            windows = [
                every(3, power, 1) + every(3, again, 1) + every(1, products, 1) + every(3, power, 2) + every(3, again, 2) + firsts,
                every(1, scale, 0) + every(1, project, 1) + every(2, align, 2, 1) + every(1, products, 2)
                + every(3, power, 3) + every(3, again, 3) + middles[:4],
                every(1, scale, 1) + every(1, project, 2) + every(2, align, 3, 2) + every(1, products, 3) + middles[4:] + backs[:4],
                every(1, scale, 2) + every(1, project, 3) + backs[4:] + ends + every(2, turn_back, slice(0, 3 * SUB)),
            ]
            weights = LEAF_WEIGHTS * (SUB // LEAF)
            for m in range(MATS):
                power(m, 0)
            for m in range(MATS):
                again(m, 0)
            for m in range(MATS):
                products(m, 0)
            for j in range(len(blocks)):
                for m in range(MATS):
                    if j:
                        couple(m, j)
                    work[m] = guarded(m, square[m])
                factor(work, worst_ref, spread_out(windows[j], weights))
                inverses[j] = [work[m] for m in range(MATS)]
            for m in range(MATS):
                scale(m, len(blocks) - 1)
            bad = jnp.max(worst_ref[...]) > 0.5
            return phase + 1, jnp.where((phase == 0) & bad, 3, limit)

        lax.while_loop(lambda carry: carry[0] < carry[1], sweep, (jnp.int32(0), jnp.int32(1)))

    update_copy = pltpu.make_async_copy(update, update_out, out_sems.at[0])
    update_copy.start()
    for m in range(MATS):
        s, side = divmod(m, 2)
        target = (new_left, new_right)[side].at[s]
        semaphore = out_sems.at[1 + m]

        @pl.when(wanted[s] != 0)
        def _():
            fresh[m, :, blocks[-1]] = z[m, blocks[-1], :].T
            pltpu.make_async_copy(fresh.at[m], target, semaphore).start()

        @pl.when(wanted[s] == 0)
        def _():
            pltpu.make_async_copy((left, right)[side].at[s], target, semaphore).start()

    update_copy.wait()
    for m in range(MATS):
        s, side = divmod(m, 2)
        pltpu.make_async_copy(fresh.at[m], (new_left, new_right)[side].at[s], out_sems.at[1 + m]).wait()


def pack_kernel(table, gradient, outbox):
    @pl.loop(0, outbox.shape[0])
    def _(k):
        start = pl.multiple_of(jnp.maximum(table[k], 0) * BLOCK, BLOCK)
        piece = gradient[:, pl.ds(start, BLOCK)]
        outbox[k] = jnp.where(table[k] >= 0, piece, jnp.zeros_like(piece))


def prepare(left, right, left_gram, right_gram, first, second):
    anywhere = pl.BlockSpec(memory_space=pl.ANY)
    vmem = pl.BlockSpec(memory_space=pltpu.VMEM)
    whole = pltpu.VMEM((SLOTS, BLOCK, BLOCK), f32)
    short = pltpu.VMEM((SLOTS, BLOCK, BLOCK), bf16)
    inputs = (left, right, left_gram, right_gram, first, second)
    return pl.pallas_call(
        prepare_kernel,
        out_shape=(pltpu.VMEM((MATS, BLOCK, BLOCK), f32), whole, whole, short, short, whole, whole, whole, whole),
        in_specs=[anywhere] * len(inputs),
        out_specs=(vmem,) * 9,
        scratch_shapes=[pltpu.SemaphoreType.DMA((len(inputs),))],
        compiler_params=pltpu.CompilerParams(vmem_limit_bytes=4 * 1024 * 1024),
        cost_estimate=pl.CostEstimate(flops=8_000_000, bytes_accessed=32 * 1024 * 1024, transcendentals=0),
    )(*(pltpu.with_memory_space_constraint(x, pltpu.HBM) for x in inputs))


def step(held, wanted, grads, prepared):
    anywhere = pl.BlockSpec(memory_space=pl.ANY)
    vmem = pl.BlockSpec(memory_space=pltpu.VMEM)
    smem = pl.BlockSpec(memory_space=pltpu.SMEM)
    whole = jax.ShapeDtypeStruct((SLOTS, BLOCK, BLOCK), f32)
    return pl.pallas_call(
        step_kernel,
        out_shape=(whole, whole, whole),
        in_specs=[smem, smem, anywhere] + [vmem] * len(prepared),
        out_specs=(anywhere, anywhere, anywhere),
        scratch_shapes=[
            pltpu.VMEM((SLOTS, *grads.shape[:1], *grads.shape[2:]), bf16),
            pltpu.VMEM((SLOTS, BLOCK, BLOCK), f32),
            pltpu.VMEM((SLOTS, BLOCK, BLOCK), f32),
            pltpu.VMEM((MATS, BLOCK, BLOCK), f32),
            pltpu.VMEM((MATS, BLOCK, BLOCK), bf16),
            pltpu.VMEM((MATS, BLOCK, BLOCK), bf16),
            pltpu.VMEM((MATS, SUB, SUB), f32),
            pltpu.VMEM((MATS, SUB, SUB), f32),
            pltpu.VMEM((MATS, SUB, SUB), f32),
            pltpu.VMEM((MATS, BLOCK, BLOCK), f32),
            pltpu.VMEM((1, 128), f32),
            pltpu.SemaphoreType.DMA((SLOTS,)),
            pltpu.SemaphoreType.DMA((1 + MATS,)),
        ],
        compiler_params=pltpu.CompilerParams(vmem_limit_bytes=36 * 1024 * 1024),
    )(
        held,
        wanted,
        pltpu.with_memory_space_constraint(grads, pltpu.HBM),
        *(pltpu.with_memory_space_constraint(x, pltpu.VMEM) for x in prepared),
    )


def local(
    gradient, slot_block, refresh_target, first_moment, second_moment, left_gram, right_gram, left_basis, right_basis
):
    owners = lax.axis_size("dp")
    owner = lax.axis_index("dp")
    device = owner * lax.axis_size("tensor") + lax.axis_index("tensor")
    table = slot_block[0]
    slab = gradient.shape[2]
    vmem = pl.BlockSpec(memory_space=pltpu.VMEM)
    smem = pl.BlockSpec(memory_space=pltpu.SMEM)
    outbox = pl.pallas_call(
        pack_kernel,
        out_shape=jax.ShapeDtypeStruct((owners * SLOTS, slab, BLOCK), bf16),
        in_specs=[smem, vmem],
        out_specs=vmem,
    )(table, gradient[0, 0])
    grads = lax.all_to_all(outbox.reshape(owners, SLOTS, slab, BLOCK), "dp", 0, 0, tiled=True)
    held = (lax.dynamic_slice_in_dim(table, owner * SLOTS, SLOTS) >= 0).astype(jnp.int32)
    wanted = (lax.dynamic_slice_in_dim(refresh_target, device * SLOTS, SLOTS) >= 0).astype(jnp.int32)
    prepared = prepare(left_basis[0], right_basis[0], left_gram[0], right_gram[0], first_moment[0], second_moment[0])
    outputs = step(held, wanted, grads, prepared)
    return tuple(x[None] for x in outputs)


def solution(mesh):
    rows = P("tensor", "dp", None, None)
    return jax.shard_map(
        local,
        mesh=mesh,
        in_specs=(P("tensor", None, "dp", None), P("tensor", None), P(), rows, rows, rows, rows, rows, rows),
        out_specs=(rows, rows, rows),
        check_vma=False,
    )
```

time: 72.8 us -> 136 us (1.87)
  the two profiles are of different devices: /device:TPU:5 before, /device:TPU:3 now
where the time goes in v3:
time: 136 us
  Pallas kernels  103 us (76%)
  local copies, waits for them, and re-layouts  21 us (15%)
  starting transfers between devices  8.83 us (6%)
  waiting for transfers between devices  1.43 us (1%)
    pallas_call x1, Pallas kernels, step(): pl.pallas_call(step_kernel, out_shape=(whole, whole, whole), in_specs=[sm...  95.2 us
    unnamed x32, local copies, waits for them, and re-layouts  21 us
    all_to_all x1, starting transfers between devices, local(): lax.all_to_all(outbox.reshape(owners, SLOTS, slab, BLOCK), 'dp', 0, 0, ti...  8.83 us
    pallas_call x1, Pallas kernels, prepare(): pl.pallas_call(prepare_kernel, out_shape=(pltpu.VMEM((MATS, BLOCK, BLOCK)...  4.72 us
  transfers between devices with their start and end apart: 1, of which 1 were waited for; matrix products, arithmetic and copies ran while one was open for 1% of the time, Pallas kernels for 3%

profile of v3, /device:TPU:3, one launch (start us, length us, event | category | flops | bytes accessed | tf_op | source)
XLA Modules:
  0.0 135.8 jit_solution(1245282757011455546)
XLA Ops:
  0.6 2.6 %shard_map.112 = bf16[64,16,512]{2,1,0:T(8,128)(2,1)} custom-call(s32[64]{0:T(128)} %bitcast.22, bf16[16,16384]{1,0:T(8,128)(2,1)} %bitcast.21), custom_call_target="tpu_custom_call" | custom-call | tf_op jit(solution)/shard_map/pallas_call | solution.py:443
  3.3 8.8 %all-to-all-start = ((bf16[32,2,16,512]{3,2,1,0:T(8,128)(2,1)}), bf16[32,2,16,512]{3,2,1,0:T(8,128)(2,1)}, u32[]{:S(2)}, u32[]{:S(2)}) async-start(bf16[32,2,16,512]{3,2,1,0:T(8,128)(2,1)} %bitcast.14), calls=%async_computation | async-start | bytes 2097152 | tf_op jit(solution)/shard_map/all_to_all | solution.py:449
  12.1 0.0 copy-start.14
  12.1 0.0 copy-start.15
  12.1 4.7 %shard_map.113 = (f32[4,512,512]{2,1,0:T(8,128)S(1)}, f32[2,512,512]{2,1,0:T(8,128)S(1)}, f32[2,512,512]{2,1,0:T(8,128)S(1)}, bf16[2,512,512]{2,1,0:T(8,128)(2,1...) custom-call(f32[2,512,512]{2,1,0:T(8,128)} %bitcast.15, ...), custom_call_target="tpu_custom_call" | custom-call | flops 8000000 | bytes 33554432 | tf_op jit(solution)/shard_map/pallas_call | solution.py:388
  16.9 0.0 copy-start
  16.9 1.9 %copy-done = f32[4,512,512]{2,1,0:T(8,128)} copy-done((f32[4,512,512]{2,1,0:T(8,128)}, f32[4,512,512]{2,1,0:T(8,128)S(1)}, u32[]{:S(2)}) %copy-start) | copy-done | bytes 4194328
  18.8 0.0 copy-start.2
  18.8 1.3 copy-done.2
  20.1 0.0 copy-start.4
  20.1 1.3 copy-done.4
  21.5 0.0 copy-start.6
  21.5 1.3 copy-done.6
  22.8 0.0 copy-start.8
  22.8 1.4 copy-done.8
  24.1 0.0 copy-start.10
  24.1 1.4 copy-done.10
  25.5 0.0 copy-start.12
  25.5 1.0 copy-done.12
  26.5 0.0 copy-done.14
  26.5 0.6 fusion.held
  27.1 0.0 copy-done.15
  27.1 0.6 compare_convert_fusion.wanted
  27.6 1.4 %all-to-all-done.grads = bf16[32,2,16,512]{3,2,1,0:T(8,128)(2,1)} async-done(((bf16[32,2,16,512]{3,2,1,0:T(8,128)(2,1)}), bf16[32,2,16,512]{3,2,1,0:T(8,128)(2,1)}, u32[]{:S(2)}, u32[]{:S(2)}) %all-to-all-start) | async-done | bytes 1048608 | tf_op jit(solution)/shard_map/all_to_all | solution.py:449
  29.1 0.0 copy-start.1
  29.1 2.2 %copy-done.1 = f32[4,512,512]{2,1,0:T(8,128)S(1)} copy-done((f32[4,512,512]{2,1,0:T(8,128)S(1)}, f32[4,512,512]{2,1,0:T(8,128)}, u32[]{:S(2)}) %copy-start.1) | copy-done | bytes 4194328
  31.3 0.0 copy-start.3
  31.3 1.6 %copy-done.3 = f32[2,512,512]{2,1,0:T(8,128)S(1)} copy-done((f32[2,512,512]{2,1,0:T(8,128)S(1)}, f32[2,512,512]{2,1,0:T(8,128)}, u32[]{:S(2)}) %copy-start.3) | copy-done | bytes 2097176
  32.9 0.0 copy-start.5
  32.9 1.6 %copy-done.5 = f32[2,512,512]{2,1,0:T(8,128)S(1)} copy-done((f32[2,512,512]{2,1,0:T(8,128)S(1)}, f32[2,512,512]{2,1,0:T(8,128)}, u32[]{:S(2)}) %copy-start.5) | copy-done | bytes 2097176
  34.4 0.0 copy-start.7
  34.4 1.6 %copy-done.7 = f32[2,512,512]{2,1,0:T(8,128)S(1)} copy-done((f32[2,512,512]{2,1,0:T(8,128)S(1)}, f32[2,512,512]{2,1,0:T(8,128)}, u32[]{:S(2)}) %copy-start.7) | copy-done | bytes 2097176
  36.0 0.0 copy-start.9
  36.0 1.6 %copy-done.9 = f32[2,512,512]{2,1,0:T(8,128)S(1)} copy-done((f32[2,512,512]{2,1,0:T(8,128)S(1)}, f32[2,512,512]{2,1,0:T(8,128)}, u32[]{:S(2)}) %copy-start.9) | copy-done | bytes 2097176
  37.6 0.0 copy-start.11
  37.6 1.6 %copy-done.11 = f32[2,512,512]{2,1,0:T(8,128)S(1)} copy-done((f32[2,512,512]{2,1,0:T(8,128)S(1)}, f32[2,512,512]{2,1,0:T(8,128)}, u32[]{:S(2)}) %copy-start.11) | copy-done | bytes 2097176
  39.2 0.0 copy-start.13
  39.2 1.2 copy-done.13
  40.4 95.2 %shard_map.114 = (f32[2,512,512]{2,1,0:T(8,128)}, f32[2,512,512]{2,1,0:T(8,128)}, f32[2,512,512]{2,1,0:T(8,128)}) custom-call(s32[2]{0:T(128)} %fusion.held, s32[2]{0:T(128)} %compare_convert_fusion.wanted, bf16[32,2,16,512]{3,2,1,0:T(8,128)(2,1)} %all-to-all-done.grads, f32[4,512,512]{2,1,0:T(8,128)S(1)} %copy-done.1, ...), custom_call_target="tpu_custom_call" | custom-call | tf_op jit(solution)/shard_map/pallas_call | solution.py:404
Async XLA Ops:
  3.3 25.8 %all-to-all-start = ((bf16[32,2,16,512]{3,2,1,0:T(8,128)(2,1)}), bf16[32,2,16,512]{3,2,1,0:T(8,128)(2,1)}, u32[]{:S(2)}, u32[]{:S(2)}) async-start(bf16[32,2,16,512]{3,2,1,0:T(8,128)(2,1)} %bitcast.14), calls=%async_computation | async-start | bytes 2097152 | tf_op jit(solution)/shard_map/all_to_all | solution.py:449
  12.1 14.4 %copy-start.14 = (s32[1,64]{1,0:T(1,128)S(1)}, s32[1,64]{1,0:T(1,128)}, u32[]{:S(2)}) copy-start(s32[1,64]{1,0:T(1,128)} %param.10) | copy-start | bytes 772
  12.1 14.9 %copy-start.15 = (s32[256]{0:T(256)S(1)}, s32[256]{0:T(256)}, u32[]{:S(2)}) copy-start(s32[256]{0:T(256)} %param.11) | copy-start | bytes 3076
  16.9 2.0 %copy-start = (f32[4,512,512]{2,1,0:T(8,128)}, f32[4,512,512]{2,1,0:T(8,128)S(1)}, u32[]{:S(2)}) copy-start(f32[4,512,512]{2,1,0:T(8,128)S(1)} %get-tuple-element.15.turned) | copy-start | bytes 12582916
  18.8 1.3 copy-start.2
  20.1 1.3 copy-start.4
  21.5 1.3 copy-start.6
  22.8 1.4 %copy-start.8 = (f32[2,512,512]{2,1,0:T(8,128)}, f32[2,512,512]{2,1,0:T(8,128)S(1)}, u32[]{:S(2)}) copy-start(f32[2,512,512]{2,1,0:T(8,128)S(1)} %get-tuple-element.22.first) | copy-start | bytes 6291460
  24.1 1.4 %copy-start.10 = (f32[2,512,512]{2,1,0:T(8,128)}, f32[2,512,512]{2,1,0:T(8,128)S(1)}, u32[]{:S(2)}) copy-start(f32[2,512,512]{2,1,0:T(8,128)S(1)} %get-tuple-element.23.second) | copy-start | bytes 6291460
  25.5 1.0 copy-start.12
  29.1 2.2 %copy-start.1 = (f32[4,512,512]{2,1,0:T(8,128)S(1)}, f32[4,512,512]{2,1,0:T(8,128)}, u32[]{:S(2)}) copy-start(f32[4,512,512]{2,1,0:T(8,128)} %copy-done) | copy-start | bytes 12582916
  31.3 1.6 %copy-start.3 = (f32[2,512,512]{2,1,0:T(8,128)S(1)}, f32[2,512,512]{2,1,0:T(8,128)}, u32[]{:S(2)}) copy-start(f32[2,512,512]{2,1,0:T(8,128)} %copy-done.2) | copy-start | bytes 6291460
  32.9 1.6 %copy-start.5 = (f32[2,512,512]{2,1,0:T(8,128)S(1)}, f32[2,512,512]{2,1,0:T(8,128)}, u32[]{:S(2)}) copy-start(f32[2,512,512]{2,1,0:T(8,128)} %copy-done.4) | copy-start | bytes 6291460
  34.4 1.6 %copy-start.7 = (f32[2,512,512]{2,1,0:T(8,128)S(1)}, f32[2,512,512]{2,1,0:T(8,128)}, u32[]{:S(2)}) copy-start(f32[2,512,512]{2,1,0:T(8,128)} %copy-done.6) | copy-start | bytes 6291460
  36.0 1.6 %copy-start.9 = (f32[2,512,512]{2,1,0:T(8,128)S(1)}, f32[2,512,512]{2,1,0:T(8,128)}, u32[]{:S(2)}) copy-start(f32[2,512,512]{2,1,0:T(8,128)} %copy-done.8) | copy-start | bytes 6291460
  37.6 1.6 %copy-start.11 = (f32[2,512,512]{2,1,0:T(8,128)S(1)}, f32[2,512,512]{2,1,0:T(8,128)}, u32[]{:S(2)}) copy-start(f32[2,512,512]{2,1,0:T(8,128)} %copy-done.10) | copy-start | bytes 6291460
  39.2 1.2 copy-start.13

commit v4 on v3

--- a/solution.py
+++ b/solution.py
@@ -163,48 +163,66 @@
     return [functools.partial(run, calls) for calls in shares]
 
 
-def prepare_kernel(
-    left_in, right_in, left_gram_in, right_gram_in, first_in, second_in,
-    turned, left, right, right_high, right_low, left_gram, right_gram, first, second, sems,
-):
-    copies = [
-        pltpu.make_async_copy(source, target, sems.at[i])
-        for i, (source, target) in enumerate(
-            (
-                (left_in, left),
-                (right_in, right),
-                (left_gram_in, left_gram),
-                (right_gram_in, right_gram),
-                (first_in, first),
-                (second_in, second),
-            )
-        )
-    ]
-    for copy in copies:
-        copy.start()
-    copies[0].wait()
+def prepare_kernel(left, right, turned, right_high, right_low):
     for s in range(SLOTS):
         turned[2 * s] = left[s].T
-    copies[1].wait()
-    for s in range(SLOTS):
         turned[2 * s + 1] = right[s].T
         right_high[s], right_low[s] = split(right[s])
-    for copy in copies[2:]:
-        copy.wait()
 
 
 def step_kernel(
-    held, wanted, grads, turned, left, right, right_high, right_low, left_gram, right_gram, first, second,
+    held, wanted, grads, turned_in, left_in, right_high_in, right_low_in, left_gram_in, right_gram_in, first_in, second_in, right_in,
     update_out, new_left, new_right,
-    g, update, temp, z, a_high, a_low, work, near, square, fresh, worst_ref, in_sems, out_sems,
+    g, turned, left, right_high, right_low, left_gram, right_gram, first, second,
+    update, temp, z, a_high, a_low, work, near, square, fresh, worst_ref, in_sems, out_sems,
 ):
     halves = [slice(c, c + CHUNK) for c in range(0, BLOCK, CHUNK)]
     blocks = [slice(c, c + SUB) for c in range(0, BLOCK, SUB)]
-    g_copies = [pltpu.make_async_copy(grads.at[:, s], g.at[s], in_sems.at[s]) for s in range(SLOTS)]
-    for copy in g_copies:
+    used = []
+
+    def copy_in(source, target):
+        used.append(pltpu.make_async_copy(source, target, in_sems.at[len(used)]))
+        return used[-1]
+
+    early = [
+        [
+            copy_in(grads.at[:, s], g.at[s]),
+            copy_in(left_gram_in.at[s], left_gram.at[s]),
+            copy_in(right_gram_in.at[s], right_gram.at[s]),
+        ]
+        for s in range(SLOTS)
+    ]
+    middle = copy_in(turned_in, turned)
+    late = [
+        copy_in(source, target)
+        for source, target in (
+            (right_high_in, right_high),
+            (right_low_in, right_low),
+            (first_in, first),
+            (second_in, second),
+            (left_in, left),
+        )
+    ]
+    for copies in early:
+        for copy in copies:
+            copy.start()
+    middle.start()
+    for copy in early[0]:
+        copy.wait()
+    for copy in late:
         copy.start()
-    for copy in g_copies:
-        copy.wait()
+
+    for m in range(MATS):
+        s, side = divmod(m, 2)
+
+        @pl.when(wanted[s] == 0)
+        def _():
+            unchanged = (left_in, right_in)[side].at[s]
+            pltpu.make_async_copy(unchanged, (new_left, new_right)[side].at[s], out_sems.at[1 + m]).start()
+
+    def wait_late():
+        for copy in late:
+            copy.wait()
 
     def g_block(s):
         return g[s].reshape(BLOCK, BLOCK)
@@ -233,6 +251,11 @@
 
     @pl.when(jnp.logical_not(refresh))
     def _():
+        for copy in early[1]:
+            copy.wait()
+        middle.wait()
+        wait_late()
+
         @pl.loop(0, SLOTS)
         def _(s):
             @pl.when(held[s] == 0)
@@ -248,6 +271,9 @@
     @pl.when(refresh)
     def _():
         for s in range(SLOTS):
+            if s:
+                for copy in early[s]:
+                    copy.wait()
             gs = g_block(s)
             gt = gs.T
             for side in range(2):
@@ -256,6 +282,8 @@
                     pieces = (gs[rows], gs, NT) if side == 0 else (gt[rows], gs, NN)
                     past = (left_gram, right_gram)[side][s, rows, :]
                     a_high[m, rows, :], a_low[m, rows, :] = split(0.95 * past + 0.05 * dot(*pieces))
+
+        middle.wait()
 
         def sweep(carry):
             phase, limit = carry
@@ -335,6 +363,11 @@
                 again(m, 0)
             for m in range(MATS):
                 products(m, 0)
+
+            @pl.when(phase == 0)
+            def _():
+                wait_late()
+
             for j in range(len(blocks)):
                 for m in range(MATS):
                     if j:
@@ -361,9 +394,6 @@
             fresh[m, :, blocks[-1]] = z[m, blocks[-1], :].T
             pltpu.make_async_copy(fresh.at[m], target, semaphore).start()
 
-        @pl.when(wanted[s] == 0)
-        def _():
-            pltpu.make_async_copy((left, right)[side].at[s], target, semaphore).start()
 
     update_copy.wait()
     for m in range(MATS):
@@ -379,55 +409,45 @@
         outbox[k] = jnp.where(table[k] >= 0, piece, jnp.zeros_like(piece))
 
 
-def prepare(left, right, left_gram, right_gram, first, second):
-    anywhere = pl.BlockSpec(memory_space=pl.ANY)
+def prepare(left, right):
     vmem = pl.BlockSpec(memory_space=pltpu.VMEM)
-    whole = pltpu.VMEM((SLOTS, BLOCK, BLOCK), f32)
-    short = pltpu.VMEM((SLOTS, BLOCK, BLOCK), bf16)
-    inputs = (left, right, left_gram, right_gram, first, second)
+    short = pltpu.HBM((SLOTS, BLOCK, BLOCK), bf16)
     return pl.pallas_call(
         prepare_kernel,
-        out_shape=(pltpu.VMEM((MATS, BLOCK, BLOCK), f32), whole, whole, short, short, whole, whole, whole, whole),
-        in_specs=[anywhere] * len(inputs),
-        out_specs=(vmem,) * 9,
-        scratch_shapes=[pltpu.SemaphoreType.DMA((len(inputs),))],
-        compiler_params=pltpu.CompilerParams(vmem_limit_bytes=4 * 1024 * 1024),
-        cost_estimate=pl.CostEstimate(flops=8_000_000, bytes_accessed=32 * 1024 * 1024, transcendentals=0),
-    )(*(pltpu.with_memory_space_constraint(x, pltpu.HBM) for x in inputs))
-
-
-def step(held, wanted, grads, prepared):
+        out_shape=(pltpu.HBM((MATS, BLOCK, BLOCK), f32), short, short),
+        in_specs=[vmem, vmem],
+        out_specs=(vmem,) * 3,
+        compiler_params=pltpu.CompilerParams(vmem_limit_bytes=16 * 1024 * 1024),
+        cost_estimate=pl.CostEstimate(flops=8_000_000, bytes_accessed=10 * 1024 * 1024, transcendentals=0),
+    )(*(pltpu.with_memory_space_constraint(x, pltpu.HBM) for x in (left, right)))
+
+
+def step(held, wanted, grads, first, second, left_gram, right_gram, left, right):
     anywhere = pl.BlockSpec(memory_space=pl.ANY)
-    vmem = pl.BlockSpec(memory_space=pltpu.VMEM)
     smem = pl.BlockSpec(memory_space=pltpu.SMEM)
     whole = jax.ShapeDtypeStruct((SLOTS, BLOCK, BLOCK), f32)
+    turned, right_high, right_low = prepare(left, right)
+    large = (grads, turned, left, right_high, right_low, left_gram, right_gram, first, second, right)
+    pair = pltpu.VMEM((SLOTS, BLOCK, BLOCK), f32)
+    short_pair = pltpu.VMEM((SLOTS, BLOCK, BLOCK), bf16)
+    four = pltpu.VMEM((MATS, BLOCK, BLOCK), f32)
+    short_four = pltpu.VMEM((MATS, BLOCK, BLOCK), bf16)
+    small = pltpu.VMEM((MATS, SUB, SUB), f32)
     return pl.pallas_call(
         step_kernel,
         out_shape=(whole, whole, whole),
-        in_specs=[smem, smem, anywhere] + [vmem] * len(prepared),
+        in_specs=[smem, smem] + [anywhere] * len(large),
         out_specs=(anywhere, anywhere, anywhere),
         scratch_shapes=[
             pltpu.VMEM((SLOTS, *grads.shape[:1], *grads.shape[2:]), bf16),
-            pltpu.VMEM((SLOTS, BLOCK, BLOCK), f32),
-            pltpu.VMEM((SLOTS, BLOCK, BLOCK), f32),
-            pltpu.VMEM((MATS, BLOCK, BLOCK), f32),
-            pltpu.VMEM((MATS, BLOCK, BLOCK), bf16),
-            pltpu.VMEM((MATS, BLOCK, BLOCK), bf16),
-            pltpu.VMEM((MATS, SUB, SUB), f32),
-            pltpu.VMEM((MATS, SUB, SUB), f32),
-            pltpu.VMEM((MATS, SUB, SUB), f32),
-            pltpu.VMEM((MATS, BLOCK, BLOCK), f32),
+            four, pair, short_pair, short_pair, pair, pair, pair, pair,
+            pair, pair, four, short_four, short_four, small, small, small, four,
             pltpu.VMEM((1, 128), f32),
-            pltpu.SemaphoreType.DMA((SLOTS,)),
+            pltpu.SemaphoreType.DMA((3 * SLOTS + 6,)),
             pltpu.SemaphoreType.DMA((1 + MATS,)),
         ],
-        compiler_params=pltpu.CompilerParams(vmem_limit_bytes=36 * 1024 * 1024),
-    )(
-        held,
-        wanted,
-        pltpu.with_memory_space_constraint(grads, pltpu.HBM),
-        *(pltpu.with_memory_space_constraint(x, pltpu.VMEM) for x in prepared),
-    )
+        compiler_params=pltpu.CompilerParams(vmem_limit_bytes=52 * 1024 * 1024),
+    )(held, wanted, *(pltpu.with_memory_space_constraint(x, pltpu.HBM) for x in large))
 
 
 def local(
@@ -449,8 +469,9 @@
     grads = lax.all_to_all(outbox.reshape(owners, SLOTS, slab, BLOCK), "dp", 0, 0, tiled=True)
     held = (lax.dynamic_slice_in_dim(table, owner * SLOTS, SLOTS) >= 0).astype(jnp.int32)
     wanted = (lax.dynamic_slice_in_dim(refresh_target, device * SLOTS, SLOTS) >= 0).astype(jnp.int32)
-    prepared = prepare(left_basis[0], right_basis[0], left_gram[0], right_gram[0], first_moment[0], second_moment[0])
-    outputs = step(held, wanted, grads, prepared)
+    outputs = step(
+        held, wanted, grads, first_moment[0], second_moment[0], left_gram[0], right_gram[0], left_basis[0], right_basis[0]
+    )
     return tuple(x[None] for x in outputs)
 
 

time: 136 us -> 161 us (1.18)
  the two profiles are of different devices: /device:TPU:3 before, /device:TPU:5 now
where the time goes in v4:
time: 161 us
  Pallas kernels  139 us (86%)
  waiting for transfers between devices  10.6 us (7%)
  starting transfers between devices  8.77 us (5%)
    pallas_call x1, Pallas kernels, step(): pl.pallas_call(step_kernel, out_shape=(whole, whole, whole), in_specs=[sm...  131 us
    all_to_all x1, waiting for transfers between devices, local(): lax.all_to_all(outbox.reshape(owners, SLOTS, slab, BLOCK), 'dp', 0, 0, ti...  10.6 us
    all_to_all x1, starting transfers between devices, local(): lax.all_to_all(outbox.reshape(owners, SLOTS, slab, BLOCK), 'dp', 0, 0, ti...  8.77 us
    pallas_call x1, Pallas kernels, prepare(): pl.pallas_call(prepare_kernel, out_shape=(pltpu.HBM((MATS, BLOCK, BLOCK),...  6.09 us
  transfers between devices with their start and end apart: 1, of which 1 were waited for; matrix products, arithmetic and copies ran while one was open for 0% of the time, Pallas kernels for 4%

profile of v4, /device:TPU:5, one launch (start us, length us, event | category | flops | bytes accessed | tf_op | source)
XLA Modules:
  0.0 160.7 jit_solution(8066081174482219170)
XLA Ops:
  0.6 2.6 %shard_map.112 = bf16[64,16,512]{2,1,0:T(8,128)(2,1)} custom-call(s32[64]{0:T(128)} %bitcast.24, bf16[16,16384]{1,0:T(8,128)(2,1)} %bitcast.23), custom_call_target="tpu_custom_call" | custom-call | tf_op jit(solution)/shard_map/pallas_call | solution.py:463
  3.3 8.8 %all-to-all-start = ((bf16[32,2,16,512]{3,2,1,0:T(8,128)(2,1)}), bf16[32,2,16,512]{3,2,1,0:T(8,128)(2,1)S(1)}, u32[]{:S(2)}, u32[]{:S(2)}) async-start(bf16[32,2,16,512]{3,2,1,0:T(8,128)(2,1)} %bitcast.18), calls=%async_computation | async-start | bytes 2097152 | tf_op jit(solution)/shard_map/all_to_all | solution.py:469
  12.0 0.0 copy-start.1
  12.1 0.0 copy-start.2
  12.1 6.1 %shard_map.113 = (f32[4,512,512]{2,1,0:T(8,128)}, bf16[2,512,512]{2,1,0:T(8,128)(2,1)}, bf16[2,512,512]{2,1,0:T(8,128)(2,1)}) custom-call(f32[2,512,512]{2,1,0:T(8,128)} %bitcast.14, f32[2,512,512]{2,1,0:T(8,128)} %bitcast.16), custom_call_target="tpu_custom_call" | custom-call | flops 8000000 | bytes 10485760 | tf_op jit(solution)/shard_map/pallas_call | solution.py:415
  18.2 0.0 copy-done.1
  18.2 0.1 fusion.held
  18.2 0.0 copy-done.2
  18.2 0.1 compare_convert_fusion.wanted
  18.3 10.6 %all-to-all-done.grads = bf16[32,2,16,512]{3,2,1,0:T(8,128)(2,1)S(1)} async-done(((bf16[32,2,16,512]{3,2,1,0:T(8,128)(2,1)}), bf16[32,2,16,512]{3,2,1,0:T(8,128)(2,1)S(1)}, u32[]{:S(2)}, u32[]{:S(2)}) %all-to-all-start) | async-done | bytes 1048608 | tf_op jit(solution)/shard_map/all_to_all | solution.py:469
  29.0 0.0 copy-start
  29.0 1.0 copy-done
  29.9 130.6 %shard_map.114 = (f32[2,512,512]{2,1,0:T(8,128)}, f32[2,512,512]{2,1,0:T(8,128)}, f32[2,512,512]{2,1,0:T(8,128)}) custom-call(s32[2]{0:T(128)S(1)} %fusion.held, s32[2]{0:T(128)S(1)} %compare_convert_fusion.wanted, bf16[32,2,16,512]{3,2,1,0:T(8,128)(2,1)} %copy-done, f32[4,512,512]{2,1,0:T(8,128)} %get-tuple-element.9.turned_in, f32[2,512,512]{2,1,0:T(8,128)} %bitcast.15, ...), custom_call_target="tpu_custom_call" | custom-call | tf_op jit(solution)/shard_map/pallas_call | solution.py:436
Async XLA Ops:
  3.3 25.7 %all-to-all-start = ((bf16[32,2,16,512]{3,2,1,0:T(8,128)(2,1)}), bf16[32,2,16,512]{3,2,1,0:T(8,128)(2,1)S(1)}, u32[]{:S(2)}, u32[]{:S(2)}) async-start(bf16[32,2,16,512]{3,2,1,0:T(8,128)(2,1)} %bitcast.18), calls=%async_computation | async-start | bytes 2097152 | tf_op jit(solution)/shard_map/all_to_all | solution.py:469
  12.0 6.1 %copy-start.1 = (s32[1,64]{1,0:T(1,128)S(1)}, s32[1,64]{1,0:T(1,128)}, u32[]{:S(2)}) copy-start(s32[1,64]{1,0:T(1,128)} %param.10) | copy-start | bytes 772
  12.1 6.2 %copy-start.2 = (s32[256]{0:T(256)S(1)}, s32[256]{0:T(256)}, u32[]{:S(2)}) copy-start(s32[256]{0:T(256)} %param.11) | copy-start | bytes 3076
  29.0 1.0 copy-start

commit v5 on v4

--- a/solution.py
+++ b/solution.py
@@ -173,7 +173,7 @@
 def step_kernel(
     held, wanted, grads, turned_in, left_in, right_high_in, right_low_in, left_gram_in, right_gram_in, first_in, second_in, right_in,
     update_out, new_left, new_right,
-    g, turned, left, right_high, right_low, left_gram, right_gram, first, second,
+    g, turned, left, right, right_high, right_low, left_gram, right_gram, first, second,
     update, temp, z, a_high, a_low, work, near, square, fresh, worst_ref, in_sems, out_sems,
 ):
     halves = [slice(c, c + CHUNK) for c in range(0, BLOCK, CHUNK)]
@@ -201,6 +201,7 @@
             (first_in, first),
             (second_in, second),
             (left_in, left),
+            (right_in, right),
         )
     ]
     for copies in early:
@@ -211,14 +212,6 @@
         copy.wait()
     for copy in late:
         copy.start()
-
-    for m in range(MATS):
-        s, side = divmod(m, 2)
-
-        @pl.when(wanted[s] == 0)
-        def _():
-            unchanged = (left_in, right_in)[side].at[s]
-            pltpu.make_async_copy(unchanged, (new_left, new_right)[side].at[s], out_sems.at[1 + m]).start()
 
     def wait_late():
         for copy in late:
@@ -394,6 +387,10 @@
             fresh[m, :, blocks[-1]] = z[m, blocks[-1], :].T
             pltpu.make_async_copy(fresh.at[m], target, semaphore).start()
 
+        @pl.when(wanted[s] == 0)
+        def _():
+            pltpu.make_async_copy((left, right)[side].at[s], target, semaphore).start()
+
 
     update_copy.wait()
     for m in range(MATS):
@@ -427,7 +424,7 @@
     smem = pl.BlockSpec(memory_space=pltpu.SMEM)
     whole = jax.ShapeDtypeStruct((SLOTS, BLOCK, BLOCK), f32)
     turned, right_high, right_low = prepare(left, right)
-    large = (grads, turned, left, right_high, right_low, left_gram, right_gram, first, second, right)
+    large = (turned, left, right_high, right_low, left_gram, right_gram, first, second, right)
     pair = pltpu.VMEM((SLOTS, BLOCK, BLOCK), f32)
     short_pair = pltpu.VMEM((SLOTS, BLOCK, BLOCK), bf16)
     four = pltpu.VMEM((MATS, BLOCK, BLOCK), f32)
@@ -436,18 +433,18 @@
     return pl.pallas_call(
         step_kernel,
         out_shape=(whole, whole, whole),
-        in_specs=[smem, smem] + [anywhere] * len(large),
+        in_specs=[smem, smem, anywhere] + [anywhere] * len(large),
         out_specs=(anywhere, anywhere, anywhere),
         scratch_shapes=[
             pltpu.VMEM((SLOTS, *grads.shape[:1], *grads.shape[2:]), bf16),
-            four, pair, short_pair, short_pair, pair, pair, pair, pair,
+            four, pair, pair, short_pair, short_pair, pair, pair, pair, pair,
             pair, pair, four, short_four, short_four, small, small, small, four,
             pltpu.VMEM((1, 128), f32),
-            pltpu.SemaphoreType.DMA((3 * SLOTS + 6,)),
+            pltpu.SemaphoreType.DMA((3 * SLOTS + 7,)),
             pltpu.SemaphoreType.DMA((1 + MATS,)),
         ],
         compiler_params=pltpu.CompilerParams(vmem_limit_bytes=52 * 1024 * 1024),
-    )(held, wanted, *(pltpu.with_memory_space_constraint(x, pltpu.HBM) for x in large))
+    )(held, wanted, grads, *(pltpu.with_memory_space_constraint(x, pltpu.HBM) for x in large))
 
 
 def local(

time: 161 us -> 126 us (0.78)
  the two profiles are of different devices: /device:TPU:5 before, /device:TPU:11 now
where the time goes in v5:
time: 126 us; the launch traced here: 125 us
  Pallas kernels  106 us (84%)
  waiting for transfers between devices  8.89 us (7%)
  starting transfers between devices  8.86 us (7%)
    pallas_call x1, Pallas kernels, step(): pl.pallas_call(step_kernel, out_shape=(whole, whole, whole), in_specs=[sm...  97.2 us
    all_to_all x1, waiting for transfers between devices, local(): lax.all_to_all(outbox.reshape(owners, SLOTS, slab, BLOCK), 'dp', 0, 0, ti...  8.89 us
    all_to_all x1, starting transfers between devices, local(): lax.all_to_all(outbox.reshape(owners, SLOTS, slab, BLOCK), 'dp', 0, 0, ti...  8.86 us
    pallas_call x1, Pallas kernels, prepare(): pl.pallas_call(prepare_kernel, out_shape=(pltpu.HBM((MATS, BLOCK, BLOCK),...  6.1 us
    pallas_call x1, Pallas kernels, local(): pl.pallas_call(pack_kernel, out_shape=jax.ShapeDtypeStruct((owners * SLOT...  2.63 us
  transfers between devices with their start and end apart: 1, of which 1 were waited for; matrix products, arithmetic and copies ran while one was open for 0% of the time, Pallas kernels for 5%

profile of v5, /device:TPU:11, one launch (start us, length us, event | category | flops | bytes accessed | tf_op | source)
XLA Modules:
  0.0 124.6 jit_solution(2264237503336656650)
XLA Ops:
  0.6 2.6 %shard_map.112 = bf16[64,16,512]{2,1,0:T(8,128)(2,1)} custom-call(s32[64]{0:T(128)} %bitcast.24, bf16[16,16384]{1,0:T(8,128)(2,1)} %bitcast.23), custom_call_target="tpu_custom_call" | custom-call | tf_op jit(solution)/shard_map/pallas_call | solution.py:460
  3.3 8.9 %all-to-all-start = ((bf16[32,2,16,512]{3,2,1,0:T(8,128)(2,1)}), bf16[32,2,16,512]{3,2,1,0:T(8,128)(2,1)S(1)}, u32[]{:S(2)}, u32[]{:S(2)}) async-start(bf16[32,2,16,512]{3,2,1,0:T(8,128)(2,1)} %bitcast.18), calls=%async_computation | async-start | bytes 2097152 | tf_op jit(solution)/shard_map/all_to_all | solution.py:466
  12.1 0.0 copy-start
  12.1 0.0 copy-start.1
  12.2 6.1 %shard_map.113 = (f32[4,512,512]{2,1,0:T(8,128)}, bf16[2,512,512]{2,1,0:T(8,128)(2,1)}, bf16[2,512,512]{2,1,0:T(8,128)(2,1)}) custom-call(f32[2,512,512]{2,1,0:T(8,128)} %bitcast.14, f32[2,512,512]{2,1,0:T(8,128)} %bitcast.16), custom_call_target="tpu_custom_call" | custom-call | flops 8000000 | bytes 10485760 | tf_op jit(solution)/shard_map/pallas_call | solution.py:412
  18.3 0.0 copy-done
  18.3 0.1 fusion.held
  18.3 0.0 copy-done.1
  18.3 0.1 compare_convert_fusion.wanted
  18.4 8.9 %all-to-all-done.grads = bf16[32,2,16,512]{3,2,1,0:T(8,128)(2,1)S(1)} async-done(((bf16[32,2,16,512]{3,2,1,0:T(8,128)(2,1)}), bf16[32,2,16,512]{3,2,1,0:T(8,128)(2,1)S(1)}, u32[]{:S(2)}, u32[]{:S(2)}) %all-to-all-start) | async-done | bytes 1048608 | tf_op jit(solution)/shard_map/all_to_all | solution.py:466
  27.3 97.2 %shard_map.114 = (f32[2,512,512]{2,1,0:T(8,128)}, f32[2,512,512]{2,1,0:T(8,128)}, f32[2,512,512]{2,1,0:T(8,128)}) custom-call(s32[2]{0:T(128)S(1)} %fusion.held, s32[2]{0:T(128)S(1)} %compare_convert_fusion.wanted, bf16[32,2,16,512]{3,2,1,0:T(8,128)(2,1)S(1)} %all-to-all-done.grads, f32[4,512,512]{2,1,0:T(8,128)} %get-tuple-element.9.turned_in, ...), custom_call_target="tpu_custom_call" | custom-call | tf_op jit(solution)/shard_map/pallas_call | solution.py:433
Async XLA Ops:
  3.3 24.0 %all-to-all-start = ((bf16[32,2,16,512]{3,2,1,0:T(8,128)(2,1)}), bf16[32,2,16,512]{3,2,1,0:T(8,128)(2,1)S(1)}, u32[]{:S(2)}, u32[]{:S(2)}) async-start(bf16[32,2,16,512]{3,2,1,0:T(8,128)(2,1)} %bitcast.18), calls=%async_computation | async-start | bytes 2097152 | tf_op jit(solution)/shard_map/all_to_all | solution.py:466
  12.1 6.1 %copy-start = (s32[1,64]{1,0:T(1,128)S(1)}, s32[1,64]{1,0:T(1,128)}, u32[]{:S(2)}) copy-start(s32[1,64]{1,0:T(1,128)} %param.10) | copy-start | bytes 772
  12.1 6.2 %copy-start.1 = (s32[256]{0:T(256)S(1)}, s32[256]{0:T(256)}, u32[]{:S(2)}) copy-start(s32[256]{0:T(256)} %param.11) | copy-start | bytes 3076
